TPU v7x, 256 devices: a whole 4x4x8 slice. The times are simulated.
256 devices in a mesh: tm: 4 (over y), rows: 32 (over x_lo, z, core), rep: 2 (over x_hi).
Axes of the slice: x: 4 (x_hi: 2, x_lo: 2; x = x_hi * 2 + x_lo), y: 4, z: 8, core: 2. Of those that a mesh axis runs over, the one named last changes fastest.
Arguments:
- latent: bfloat16 [4, 16, 16, 128, 128], P('rep', None, 'tm', 'rows'), may hold values from -6 to 6
- weight: bfloat16 [384, 432], replicated, may hold values from -0.3125 to 0.3125
- cotangent: bfloat16 [4, 384, 16, 128, 128], P('rep', None, 'tm', 'rows'), may hold values from -6 to 6
- frame_group_index: int32 [4, 16], P('rep'), may hold values from 0 to 2, never falling along the last dimension, each value on 1 to 8 neighbouring positions
- sequence_token_order: int32 [65536], replicated, may hold values from 0 to 65535, as said below
Outputs:
- sequence_token_gradient: bfloat16 [4, 32768, 128], P('rep', ('tm', 'rows'))
- weight_gradient: float32 [384, 432], replicated
Inputs may be any that keep to these rules, and one draw needn't show every extreme that they name: `frame_group_index`: Frame-group numbers never fall along a clip's frames. A permutation of a clip's tokens. Call the tokens of frames t * 4 to t * 4 + 3 and half-rows r * (2) to r * 2 + 4 // 2 - 1 the block of (t, r), numbered t * 32 + r; every 512 positions in a row of sequence_token_order (positions j * 512 onward) hold exactly 4 tokens of every block.
All inputs are finite; a program needn't handle non-finite values.
Results may differ from a plain program's by a relative error of at most 0.0065.
Values may be sent and summed in bfloat16 or wider, within the bound.
No kernel may reach another device: no remote copies, remote signals or barrier semaphores. Data moves between devices by JAX's collectives and lax.ppermute only.
A program may use at most 128 MiB of HBM per device.

v0:
```python
import math

import jax
import jax.numpy as jnp
from jax import lax
from jax.experimental import pallas as pl
from jax.experimental.pallas import tpu as pltpu
from jax.sharding import Mesh, PartitionSpec as P

BF = jnp.bfloat16
F32 = jnp.float32
BAND = ("xl", "z", "core")
PEERS = ("tm", "xl", "z", "core")
NT = (((1,), (1,)), ((), ()))
VMEM = 48 * 1024 * 1024


def matmul(a, b):
    return jnp.dot(a, b, preferred_element_type=F32)


def matmul_nt(a, b):
    return lax.dot_general(a, b, NT, preferred_element_type=F32)


def call(body, outs, cost, scratch=(), grid=None, in_specs=None, out_specs=None):
    params = {}
    if grid is not None:
        params = {"grid": grid, "in_specs": in_specs, "out_specs": out_specs}
    elif in_specs is not None:
        params = {"in_specs": in_specs}
    return pl.pallas_call(
        body,
        out_shape=outs,
        scratch_shapes=list(scratch),
        cost_estimate=pl.CostEstimate(flops=int(cost[0]), bytes_accessed=int(cost[1]), transcendentals=0),
        compiler_params=pltpu.CompilerParams(vmem_limit_bytes=VMEM),
        **params,
    )


def ones_where(cond):
    return jnp.where(cond, 1.0, 0.0).astype(BF)


def select_body(me_ref, order_ref, own_ref, pair_ref, send_ref, take_ref):
    me = me_ref[0]
    order = order_ref[...]
    frame = order >> 12
    row = (order >> 6) & 63
    mine = ((frame >> 2) * 32 + (row >> 1)) == me
    local_id = ((frame & 3) * 2 + (row & 1)) * 64 + (order & 63)
    up = lax.broadcasted_iota(jnp.int32, (512, 512), 0)
    lane = lax.broadcasted_iota(jnp.int32, (512, 512), 1)
    running = matmul(ones_where(mine), ones_where(up <= lane))
    spread = ones_where(
        (lax.broadcasted_iota(jnp.int32, (512, 128), 0) >> 2)
        == lax.broadcasted_iota(jnp.int32, (512, 128), 1)
    )
    slot = lax.broadcasted_iota(jnp.int32, (512, 1), 0) & 3
    source = jnp.zeros((512, 1), F32)
    for s in range(4):
        hit = mine & (running == s + 1.0)
        value = jnp.sum(jnp.where(hit, local_id, 0).astype(F32), axis=1, keepdims=True)
        high = jnp.floor(value * (1.0 / 16.0))
        low = value - high * 16.0
        high = matmul(spread, jnp.broadcast_to(high, (128, 128)).astype(BF))
        low = matmul(spread, jnp.broadcast_to(low, (128, 128)).astype(BF))
        source = source + jnp.where(slot == s, (high * 16.0 + low)[:, 0:1], 0.0)
    place = 2 * source.astype(jnp.int32)
    send_ref[...] = ones_where(lax.broadcasted_iota(jnp.int32, (512, 1024), 1) == place)
    own = own_ref[...]
    sender = (own >> 14) * 32 + ((own >> 7) & 31)
    pairs = pair_ref[...]
    pos = lax.broadcasted_iota(jnp.int32, (256, 512), 1)
    half = lax.broadcasted_iota(jnp.int32, (256, 512), 0)
    for e in range(2):
        mate = pairs[:, e : e + 1]
        mate = (mate >> 14) * 32 + ((mate >> 7) & 31)
        earlier = (sender == mate) & (pos < 2 * half + e)
        count = jnp.sum(jnp.where(earlier, 1.0, 0.0), axis=1, keepdims=True)
        take_ref[e] = ones_where(pos == mate * 4 + count.astype(jnp.int32))


def main_body(
    tm_ref, seg_ref, prev_ref, lat_ref, low_ref, high_ref, cot_ref, w_ref, wt_ref,
    wg_ref, own_ref, glow_ref, ghigh_ref, gprev_ref,
    ext, patch, total, spread,
):
    b = pl.program_id(0)
    f = pl.program_id(1)
    lanes = lax.broadcasted_iota(jnp.int32, (1, 128), 1)

    @pl.when((b == 0) & (f == 0))
    def _():
        patch[432:512, :] = jnp.zeros((80, 512), BF)
        total[...] = jnp.zeros_like(total)

    @pl.when(f == 0)
    def _():
        spread[...] = jnp.zeros_like(spread)
        ext[1, 0:2, 1:5] = prev_ref[0]
        ext[1, 2:6, 1:5] = lat_ref[0]
        ext[1, :, 0] = low_ref[0]
        ext[1, :, 5] = high_ref[0]
        for fr in range(6):
            x = ext[1, fr].astype(F32).reshape(96, 128)
            left = jnp.where(lanes == 0, 0.0, pltpu.roll(x, 1, 1))
            right = jnp.where(lanes == 127, 0.0, pltpu.roll(x, 127, 1))
            ext[0, fr] = left.astype(BF).reshape(6, 16, 128)
            ext[2, fr] = right.astype(BF).reshape(6, 16, 128)

    frame = tm_ref[0] * 4 + f
    seg = seg_ref[b, frame]
    factors = []
    for a in range(3):
        before = frame - (2 - a)
        same = (before >= 0) & (seg_ref[b, jnp.maximum(before, 0)] == seg)
        factors.append(jnp.where(same, 1.0, 0.0))
    for a in range(3):
        mask = jnp.full((16, 128), factors[a], F32).astype(BF)
        for r in range(3):
            for c in range(3):
                top = (a * 9 + r * 3 + c) * 16
                for h in range(4):
                    patch[top : top + 16, h * 128 : h * 128 + 128] = ext[c, f + a, h + r] * mask
    patches = patch[...]
    pre = matmul(w_ref[...], patches)
    sig = 0.5 * jnp.tanh(0.5 * pre) + 0.5
    grad = (cot_ref[0].astype(F32) * sig * (1.0 + pre * (1.0 - sig))).astype(BF)
    total[...] += matmul_nt(grad, patches)
    back = matmul(wt_ref[...], grad)
    for a in range(3):
        for c in range(3):
            for row in range(6):
                acc = None
                for r in range(3):
                    h = row - r
                    if 0 <= h < 4:
                        top = (a * 9 + r * 3 + c) * 16
                        term = back[top : top + 16, h * 128 : h * 128 + 128]
                        acc = term if acc is None else acc + term
                spread[c, f + a, row] += acc * factors[a]

    @pl.when(f == 3)
    def _():
        for fr in range(6):
            x0 = spread[0, fr].reshape(96, 128)
            x2 = spread[2, fr].reshape(96, 128)
            x = (
                spread[1, fr].reshape(96, 128)
                + jnp.where(lanes == 127, 0.0, pltpu.roll(x0, 127, 1))
                + jnp.where(lanes == 0, 0.0, pltpu.roll(x2, 1, 1))
            ).reshape(6, 16, 128)
            glow_ref[0, fr] = x[0].astype(BF)
            ghigh_ref[0, fr] = x[5].astype(BF)
            if fr < 2:
                gprev_ref[0, fr] = x[1:5]
            else:
                own_ref[0, fr - 2] = x[1:5]

    @pl.when((b == 1) & (f == 3))
    def _():
        wg_ref[...] = total[...].astype(wg_ref.dtype)


def out_body(own_ref, low_ref, high_ref, next_ref, send_ref, out_ref, rows):
    for b in range(2):
        for f in range(4):
            for h in range(4):
                x = own_ref[b, f, h]
                if h == 0:
                    x = x + low_ref[b, 2 + f].astype(F32)
                if h == 3:
                    x = x + high_ref[b, 2 + f].astype(F32)
                if f >= 2:
                    x = x + next_ref[b, f - 2, h].astype(F32)
                x = x.astype(BF)
                top = (b * 2 + h % 2) * 16
                col = (f * 2 + h // 2) * 128
                rows[top : top + 16, col : col + 128] = x
                rows[64 + top : 80 + top, col : col + 128] = pltpu.roll(x.astype(F32), 127, 1).astype(BF)
    out_ref[...] = matmul_nt(send_ref[...], rows[...]).astype(BF)


def take_body(got_ref, take_ref, out_ref):
    src = lax.broadcasted_iota(jnp.int32, (128, 128), 0)
    dst = lax.broadcasted_iota(jnp.int32, (128, 128), 1)
    want = ((dst & 1) << 6) + (((dst >> 1) & 1) << 4) + ((dst >> 2) & 15)
    got = got_ref[...]
    for b in range(2):
        total = None
        for e in range(2):
            place = ones_where((src == want + b * 32) & ((dst >> 6) == e))
            moved = matmul(got, place).astype(BF)
            term = matmul(take_ref[e], moved)
            total = term if total is None else total + term
        out_ref[b] = total.astype(BF)


def reduce_weight(wg):
    every = ("rep",) + PEERS
    parts = exchange(wg.reshape(256, 6, 128), every)
    part = jnp.sum(parts.astype(F32), axis=0).astype(BF)
    whole_sum = exchange(jnp.broadcast_to(part[None], (256, 6, 128)), every)
    cells = math.sqrt(4 * 16 * 128 * 128)
    return whole_sum.reshape(384, 512)[:, :432].astype(F32) * (1.0 / cells)


def shifted(value, axes, step):
    count = math.prod(lax.axis_size(a) for a in axes)
    pairs = [(i, i + step) for i in range(count) if 0 <= i + step < count]
    return lax.ppermute(value, axes, pairs)


def exchange(value, axes):
    return lax.all_to_all(value, axes, split_axis=0, concat_axis=0, tiled=True)


def whole(shape):
    return pl.BlockSpec(shape, lambda b, f: (0,) * len(shape))


def on_device(latent, weight, cotangent, groups, order):
    tm = lax.axis_index("tm")
    band = lax.axis_index(BAND)
    me = tm * 32 + band
    smem = pl.BlockSpec(memory_space=pltpu.SMEM)
    vmem = pl.BlockSpec(memory_space=pltpu.VMEM)
    lat = latent.transpose(0, 2, 3, 1, 4)
    prev = shifted(lat[:, 2:4], ("tm",), 1)
    low = shifted(jnp.concatenate([prev[:, :, 3], lat[:, :, 3]], axis=1), BAND, 1)
    high = shifted(jnp.concatenate([prev[:, :, 0], lat[:, :, 0]], axis=1), BAND, -1)
    rows = order.reshape(128, 512)
    own = lax.dynamic_slice_in_dim(rows, me, 1, axis=0)
    send, take = call(
        select_body,
        (jax.ShapeDtypeStruct((512, 1024), BF), jax.ShapeDtypeStruct((2, 256, 512), BF)),
        (500e6, 2e6),
        in_specs=[smem, vmem, vmem, vmem],
    )(me.reshape(1), rows, own, own.reshape(256, 2))
    cot = cotangent.reshape(2, 384, 2048)
    padded = jnp.pad(weight, ((0, 0), (0, 80)))
    per_clip = lambda *shape: pl.BlockSpec((1,) + shape, lambda b, f: (b,) + (0,) * len(shape))
    wg, grad, glow, ghigh, gprev = call(
        main_body,
        (
            jax.ShapeDtypeStruct((384, 512), BF),
            jax.ShapeDtypeStruct((2, 4, 4, 16, 128), F32),
            jax.ShapeDtypeStruct((2, 6, 16, 128), BF),
            jax.ShapeDtypeStruct((2, 6, 16, 128), BF),
            jax.ShapeDtypeStruct((2, 2, 4, 16, 128), F32),
        ),
        (4.5e9, 5e6),
        scratch=[
            pltpu.VMEM((3, 6, 6, 16, 128), BF),
            pltpu.VMEM((512, 512), BF),
            pltpu.VMEM((384, 512), F32),
            pltpu.VMEM((3, 6, 6, 16, 128), F32),
        ],
        grid=(2, 4),
        in_specs=[
            smem,
            smem,
            per_clip(2, 4, 16, 128),
            per_clip(4, 4, 16, 128),
            per_clip(6, 16, 128),
            per_clip(6, 16, 128),
            pl.BlockSpec((1, 384, 512), lambda b, f: (b, 0, f)),
            whole((384, 512)),
            whole((432, 384)),
        ],
        out_specs=[
            whole((384, 512)),
            per_clip(4, 4, 16, 128),
            per_clip(6, 16, 128),
            per_clip(6, 16, 128),
            per_clip(2, 4, 16, 128),
        ],
    )(tm.reshape(1), groups, prev, lat, low, high, cot, padded, weight.T)
    weight_gradient = reduce_weight(wg)
    from_low = shifted(ghigh, BAND, 1)
    from_high = shifted(glow, BAND, -1)
    early = gprev.at[:, :, 0].add(from_low[:, 0:2].astype(F32))
    early = early.at[:, :, 3].add(from_high[:, 0:2].astype(F32)).astype(BF)
    from_next = shifted(early, ("tm",), -1)
    outgoing = call(
        out_body,
        jax.ShapeDtypeStruct((512, 128), BF),
        (150e6, 2e6),
        scratch=[pltpu.VMEM((128, 1024), BF)],
        in_specs=[vmem] * 5,
    )(grad, from_low, from_high, from_next, send)
    got = exchange(outgoing.reshape(128, 4, 128), PEERS).reshape(512, 128)
    tokens = call(
        take_body,
        jax.ShapeDtypeStruct((2, 256, 128), BF),
        (200e6, 1e6),
        in_specs=[vmem] * 2,
    )(got, take)
    return tokens, weight_gradient


def solution(mesh):
    split = Mesh(mesh.devices.reshape(4, 2, 8, 2, 2), ("tm", "xl", "z", "core", "rep"))
    placed = P("rep", None, "tm", BAND, None)
    return jax.shard_map(
        on_device,
        mesh=split,
        in_specs=(placed, P(), placed, P("rep", None), P()),
        out_specs=(P("rep", PEERS, None), P()),
        check_vma=False,
    )
```

profile of v0, /device:TPU:1, one launch (start us, length us, event | category | flops | bytes accessed | tf_op | source)
XLA Modules:
  0.0 134.8 jit_solution(11324796565763453111)
XLA Ops:
  0.6 0.9 copy.20
  1.6 4.0 %collective-permute-start = (bf16[2,2,4,16,128]{4,3,1,0,2:T(8,128)(2,1)S(1)}, bf16[2,2,4,16,128]{4,3,1,0,2:T(8,128)(2,1)S(1)}, u32[]{:S(2)}, u32[]{:S(2)}) collective-permute-start(bf16[2,2,4,16,128]{4,3,1,0,2:T(8,128)(2,1)S(1)} %slice.98), channel_id=1, source_target_pairs={{0,64},{64,128},{128,192},{1,65},{65,129},{129,193},{2,66},{66,130... | collective-permute-start | bytes 196616 | tf_op jit(solution)/shard_map/ppermute | solution.py:213
  5.6 1.3 collective-permute-done
  6.9 0.0 copy-start.11
  6.9 0.6 copy-done.11
  7.6 0.6 pad_maximum_fusion
  8.2 4.9 %collective-permute-start.1 = (bf16[2,6,16,128]{3,2,1,0:T(8,128)(2,1)}, bf16[2,6,16,128]{3,2,1,0:T(8,128)(2,1)S(1)}, u32[]{:S(2)}, u32[]{:S(2)}) collective-permute-start(bf16[2,6,16,128]{3,2,1,0:T(8,128)(2,1)} %pad_maximum_fusion), channel_id=1, source_target_pairs={{0,2},{2,4},{4,6},{6,8},{8,10},{10,12},{12,14},{14,16},{16,18},{18... | collective-permute-start | bytes 147464 | tf_op jit(solution)/shard_map/ppermute | solution.py:213
  13.1 0.6 pad_maximum_fusion.1
  13.7 1.9 %collective-permute-start.2 = (bf16[2,6,16,128]{3,2,1,0:T(8,128)(2,1)}, bf16[2,6,16,128]{3,2,1,0:T(8,128)(2,1)}, u32[]{:S(2)}, u32[]{:S(2)}) collective-permute-start(bf16[2,6,16,128]{3,2,1,0:T(8,128)(2,1)} %pad_maximum_fusion.1), channel_id=1, source_target_pairs={{2,0},{4,2},{6,4},{8,6},{10,8},{12,10},{14,12},{16,14},{18,16},{20... | collective-permute-start | bytes 147464 | tf_op jit(solution)/shard_map/ppermute | solution.py:213
  15.7 1.6 %copy.19 = bf16[2,16,4,4,128]{4,1,3,2,0:T(8,128)(2,1)} copy(bf16[2,16,4,4,128]{4,3,2,1,0:T(4,128)(2,1)} %param.9) | data formatting | bytes 262144 | tf_op jit(solution)/shard_map/transpose | solution.py:230
  17.3 0.0 copy-start
  17.3 0.0 copy-start.10
  17.3 4.8 %reshape.117.cot_ref = bf16[2,384,2048]{2,1,0:T(8,128)(2,1)S(1)} reshape(bf16[2,384,4,4,128]{4,3,2,1,0:T(4,128)(2,1)} %param.11) | data formatting | bytes 6291456 | tf_op jit(solution)/shard_map/reshape | solution.py:242
  22.1 0.0 copy-done
  22.1 0.9 copy.12
  23.0 1.0 pad.8.w_ref
  24.1 0.8 copy.13.prev_ref
  24.9 0.0 collective-permute-done.1.low_ref
  24.9 0.0 copy-start.8
  24.9 0.6 copy-done.8
  25.5 0.0 collective-permute-done.2.high_ref
  25.5 0.0 copy-done.10
  25.5 0.0 copy-start.1
  25.5 1.0 copy-done.1
  26.5 0.0 copy-start.5
  26.5 0.9 copy-done.5
  27.4 0.0 copy-start.9
  27.4 0.8 copy-done.9
  28.2 10.7 %shard_map.68 = (bf16[384,512]{1,0:T(8,128)(2,1)S(1)}, f32[2,4,4,16,128]{4,3,2,1,0:T(8,128)S(1)}, bf16[2,6,16,128]{3,2,1,0:T(8,128)(2,1)S(1)}, bf16[2,6,16,128]{...) custom-call(s32[1]{0:T(128)} %bitcast.tm_ref, s32[2,16]{1,0:T(2,128)S(1)} %copy-done.10, ...), custom_call_target="tpu_custom_call" | custom-call | flops 4499999744 | bytes 5000000 | tf_op jit(solution)/shard_map/pallas_call | solution.py:245
  38.9 0.0 copy-start.2
  38.9 0.6 copy-done.2
  39.6 0.0 copy-start.3
  39.6 0.7 copy-done.3
  40.3 0.6 copy-done.6
  40.9 0.6 copy-done.7
  41.5 1.1 reshape.125
  42.6 16.3 %all-to-all-start.1 = ((bf16[256,6,128]{2,1,0:T(8,128)(2,1)}), bf16[256,6,128]{2,1,0:T(8,128)(2,1)S(1)}, u32[]{:S(2)}, u32[]{:S(2)}) async-start(bf16[256,6,128]{2,1,0:T(8,128)(2,1)} %reshape.125), calls=%async_computation.1 | async-start | bytes 1048576 | tf_op jit(solution)/shard_map/all_to_all | solution.py:217
  59.0 3.7 %collective-permute-start.3 = (bf16[2,6,16,128]{3,2,1,0:T(8,128)(2,1)}, bf16[2,6,16,128]{3,2,1,0:T(8,128)(2,1)S(1)}, u32[]{:S(2)}, u32[]{:S(2)}) collective-permute-start(bf16[2,6,16,128]{3,2,1,0:T(8,128)(2,1)} %copy-done.7), channel_id=1, source_target_pairs={{0,2},{2,4},{4,6},{6,8},{8,10},{10,12},{12,14},{14,16},{16,18},{18... | collective-permute-start | bytes 147464 | tf_op jit(solution)/shard_map/ppermute | solution.py:213
  62.7 1.0 reshape.121.order_ref
  63.7 1.9 %collective-permute-start.4 = (bf16[2,6,16,128]{3,2,1,0:T(8,128)(2,1)}, bf16[2,6,16,128]{3,2,1,0:T(8,128)(2,1)S(1)}, u32[]{:S(2)}, u32[]{:S(2)}) collective-permute-start(bf16[2,6,16,128]{3,2,1,0:T(8,128)(2,1)} %copy-done.6), channel_id=1, source_target_pairs={{2,0},{4,2},{6,4},{8,6},{10,8},{12,10},{14,12},{16,14},{18,16},{20... | collective-permute-start | bytes 147464 | tf_op jit(solution)/shard_map/ppermute | solution.py:213
  65.6 0.0 collective-permute-done.3.low_ref
  65.6 1.4 %fusion.1 = f32[2,2,4,16,128]{4,3,2,1,0:T(8,128)} fusion(f32[2,2,4,16,128]{4,3,2,1,0:T(8,128)} %copy-done.2, bf16[2,6,16,128]{3,2,1,0:T(8,128)(2,1)S(1)} %collective-permute-done.3.low_ref), kind=kLoop, calls=%fused_computation.10 | loop fusion | flops 16384 | bytes 81920 | tf_op jit(solution)/shard_map/scatter-add | solution.py:284
  67.0 4.8 %collective-permute-done.4.high_ref = bf16[2,6,16,128]{3,2,1,0:T(8,128)(2,1)S(1)} collective-permute-done((bf16[2,6,16,128]{3,2,1,0:T(8,128)(2,1)}, bf16[2,6,16,128]{3,2,1,0:T(8,128)(2,1)S(1)}, u32[]{:S(2)}, u32[]{:S(2)}) %collective-permute-start.4) | collective-permute-done | bytes 49184 | tf_op jit(solution)/shard_map/ppermute | solution.py:213
  71.8 1.4 %fusion = f32[2,2,4,16,128]{4,3,2,1,0:T(8,128)} fusion(f32[2,2,4,16,128]{4,3,2,1,0:T(8,128)} %fusion.1, bf16[2,6,16,128]{3,2,1,0:T(8,128)(2,1)S(1)} %collective-permute-done.4.high_ref), kind=kLoop, calls=%fused_computation.6 | loop fusion | flops 16384 | bytes 81920 | tf_op jit(solution)/shard_map/scatter-add | solution.py:285
  73.2 0.9 convert_element_type.6
  74.1 1.3 collective-permute-start.5
  75.4 0.5 broadcast.50
  75.9 0.7 fusion.2
  76.6 0.1 reshape.122.pair_ref
  76.7 1.3 shard_map.69
  78.1 1.4 %collective-permute-done.5.next_ref = bf16[2,2,4,16,128]{4,3,2,1,0:T(8,128)(2,1)S(1)} collective-permute-done((bf16[2,2,4,16,128]{4,3,2,1,0:T(8,128)(2,1)S(1)}, bf16[2,2,4,16,128]{4,3,2,1,0:T(8,128)(2,1)S(1)}, u32[]{:S(2)}, u32[]{:S(2)}) %collective-permute-start.5) | collective-permute-done | bytes 65568 | tf_op jit(solution)/shard_map/ppermute | solution.py:213
  79.5 0.0 copy-done.4
  79.5 1.2 shard_map.70
  80.6 0.0 all-to-all-done.1
  80.6 13.8 %all-to-all-start = ((bf16[128,4,128]{2,1,0:T(4,128)(2,1)}), bf16[128,4,128]{2,1,0:T(4,128)(2,1)S(1)}, u32[]{:S(2)}, u32[]{:S(2)}) async-start(bf16[128,4,128]{2,1,0:T(4,128)(2,1)} %bitcast.11), calls=%async_computation | async-start | bytes 262144 | tf_op jit(solution)/shard_map/all_to_all | solution.py:217
  94.4 0.3 reduce_sum.12
  94.7 11.8 %all-to-all-done = bf16[128,4,128]{2,1,0:T(4,128)(2,1)S(1)} async-done(((bf16[128,4,128]{2,1,0:T(4,128)(2,1)}), bf16[128,4,128]{2,1,0:T(4,128)(2,1)S(1)}, u32[]{:S(2)}, u32[]{:S(2)}) %all-to-all-start) | async-done | bytes 131104 | tf_op jit(solution)/shard_map/all_to_all | solution.py:217
  106.6 0.9 broadcast_in_dim.2
  107.4 5.9 %all-to-all-start.2 = ((bf16[256,6,128]{2,1,0:T(8,128)(2,1)}), bf16[256,6,128]{2,1,0:T(8,128)(2,1)S(1)}, u32[]{:S(2)}, u32[]{:S(2)}) async-start(bf16[256,6,128]{2,1,0:T(8,128)(2,1)} %broadcast_in_dim.2), calls=%async_computation.2 | async-start | bytes 1048576 | tf_op jit(solution)/shard_map/all_to_all | solution.py:217
  113.3 1.5 %shard_map.71 = bf16[2,256,128]{2,1,0:T(8,128)(2,1)} custom-call(bf16[512,128]{1,0:T(8,128)(2,1)S(1)} %bitcast.29, bf16[2,256,512]{2,1,0:T(8,128)(2,1)S(1)} %get-tuple-element.38.take_ref), custom_call_target="tpu_custom_call" | custom-call | flops 200000000 | bytes 1000000 | tf_op jit(solution)/shard_map/pallas_call | solution.py:295
  114.8 18.5 %all-to-all-done.2 = bf16[256,6,128]{2,1,0:T(8,128)(2,1)S(1)} async-done(((bf16[256,6,128]{2,1,0:T(8,128)(2,1)}), bf16[256,6,128]{2,1,0:T(8,128)(2,1)S(1)}, u32[]{:S(2)}, u32[]{:S(2)}) %all-to-all-start.2) | async-done | bytes 393248 | tf_op jit(solution)/shard_map/all_to_all | solution.py:217
  133.3 0.3 reshape.126
  133.6 0.1 convert_multiply_fusion
  133.7 1.1 copy.15
  (6 shorter events, 0.0 us)
Async XLA Ops:
  1.6 5.4 %collective-permute-start = (bf16[2,2,4,16,128]{4,3,1,0,2:T(8,128)(2,1)S(1)}, bf16[2,2,4,16,128]{4,3,1,0,2:T(8,128)(2,1)S(1)}, u32[]{:S(2)}, u32[]{:S(2)}) collective-permute-start(bf16[2,2,4,16,128]{4,3,1,0,2:T(8,128)(2,1)S(1)} %slice.98), channel_id=1, source_target_pairs={{0,64},{64,128},{128,192},{1,65},{65,129},{129,193},{2,66},{66,130... | collective-permute-start | bytes 196616 | tf_op jit(solution)/shard_map/ppermute | solution.py:213
  6.9 0.6 copy-start.11
  8.2 16.7 %collective-permute-start.1 = (bf16[2,6,16,128]{3,2,1,0:T(8,128)(2,1)}, bf16[2,6,16,128]{3,2,1,0:T(8,128)(2,1)S(1)}, u32[]{:S(2)}, u32[]{:S(2)}) collective-permute-start(bf16[2,6,16,128]{3,2,1,0:T(8,128)(2,1)} %pad_maximum_fusion), channel_id=1, source_target_pairs={{0,2},{2,4},{4,6},{6,8},{8,10},{10,12},{12,14},{14,16},{16,18},{18... | collective-permute-start | bytes 147464 | tf_op jit(solution)/shard_map/ppermute | solution.py:213
  13.7 11.8 %collective-permute-start.2 = (bf16[2,6,16,128]{3,2,1,0:T(8,128)(2,1)}, bf16[2,6,16,128]{3,2,1,0:T(8,128)(2,1)}, u32[]{:S(2)}, u32[]{:S(2)}) collective-permute-start(bf16[2,6,16,128]{3,2,1,0:T(8,128)(2,1)} %pad_maximum_fusion.1), channel_id=1, source_target_pairs={{2,0},{4,2},{6,4},{8,6},{10,8},{12,10},{14,12},{16,14},{18,16},{20... | collective-permute-start | bytes 147464 | tf_op jit(solution)/shard_map/ppermute | solution.py:213
  17.3 4.8 %copy-start = (bf16[384,432]{0,1:T(8,128)(2,1)S(1)}, bf16[384,432]{0,1:T(8,128)(2,1)}, u32[]{:S(2)}) copy-start(bf16[384,432]{0,1:T(8,128)(2,1)} %param.10) | copy-start | bytes 995332
  17.3 8.3 %copy-start.10 = (s32[2,16]{1,0:T(2,128)S(1)}, s32[2,16]{1,0:T(2,128)}, u32[]{:S(2)}) copy-start(s32[2,16]{1,0:T(2,128)} %seg_ref.1) | copy-start | bytes 388
  24.9 0.6 copy-start.8
  25.5 1.0 copy-start.1
  26.5 0.9 copy-start.5
  27.4 0.8 copy-start.9
  38.9 0.7 copy-start.2
  39.6 0.7 copy-start.3
  40.3 0.6 copy-start.6
  40.9 0.6 copy-start.7
  41.5 38.0 %copy-start.4 = (f32[2,4,4,16,128]{4,3,2,1,0:T(8,128)S(1)}, f32[2,4,4,16,128]{4,3,2,1,0:T(8,128)}, u32[]{:S(2)}) copy-start(f32[2,4,4,16,128]{4,3,2,1,0:T(8,128)} %copy-done.3) | copy-start | bytes 786436
  42.6 38.0 %all-to-all-start.1 = ((bf16[256,6,128]{2,1,0:T(8,128)(2,1)}), bf16[256,6,128]{2,1,0:T(8,128)(2,1)S(1)}, u32[]{:S(2)}, u32[]{:S(2)}) async-start(bf16[256,6,128]{2,1,0:T(8,128)(2,1)} %reshape.125), calls=%async_computation.1 | async-start | bytes 1048576 | tf_op jit(solution)/shard_map/all_to_all | solution.py:217
  59.0 6.6 %collective-permute-start.3 = (bf16[2,6,16,128]{3,2,1,0:T(8,128)(2,1)}, bf16[2,6,16,128]{3,2,1,0:T(8,128)(2,1)S(1)}, u32[]{:S(2)}, u32[]{:S(2)}) collective-permute-start(bf16[2,6,16,128]{3,2,1,0:T(8,128)(2,1)} %copy-done.7), channel_id=1, source_target_pairs={{0,2},{2,4},{4,6},{6,8},{8,10},{10,12},{12,14},{14,16},{16,18},{18... | collective-permute-start | bytes 147464 | tf_op jit(solution)/shard_map/ppermute | solution.py:213
  63.7 8.1 %collective-permute-start.4 = (bf16[2,6,16,128]{3,2,1,0:T(8,128)(2,1)}, bf16[2,6,16,128]{3,2,1,0:T(8,128)(2,1)S(1)}, u32[]{:S(2)}, u32[]{:S(2)}) collective-permute-start(bf16[2,6,16,128]{3,2,1,0:T(8,128)(2,1)} %copy-done.6), channel_id=1, source_target_pairs={{2,0},{4,2},{6,4},{8,6},{10,8},{12,10},{14,12},{16,14},{18,16},{20... | collective-permute-start | bytes 147464 | tf_op jit(solution)/shard_map/ppermute | solution.py:213
  74.1 5.3 %collective-permute-start.5 = (bf16[2,2,4,16,128]{4,3,2,1,0:T(8,128)(2,1)S(1)}, bf16[2,2,4,16,128]{4,3,2,1,0:T(8,128)(2,1)S(1)}, u32[]{:S(2)}, u32[]{:S(2)}) collective-permute-start(bf16[2,2,4,16,128]{4,3,2,1,0:T(8,128)(2,1)S(1)} %convert_element_type.6), channel_id=1, source_target_pairs={{64,0},{128,64},{192,128},{65,1},{129,65},{193,129},{66,2},{130,66... | collective-permute-start | bytes 196616 | tf_op jit(solution)/shard_map/ppermute | solution.py:213
  80.6 25.9 %all-to-all-start = ((bf16[128,4,128]{2,1,0:T(4,128)(2,1)}), bf16[128,4,128]{2,1,0:T(4,128)(2,1)S(1)}, u32[]{:S(2)}, u32[]{:S(2)}) async-start(bf16[128,4,128]{2,1,0:T(4,128)(2,1)} %bitcast.11), calls=%async_computation | async-start | bytes 262144 | tf_op jit(solution)/shard_map/all_to_all | solution.py:217
  107.4 25.9 %all-to-all-start.2 = ((bf16[256,6,128]{2,1,0:T(8,128)(2,1)}), bf16[256,6,128]{2,1,0:T(8,128)(2,1)S(1)}, u32[]{:S(2)}, u32[]{:S(2)}) async-start(bf16[256,6,128]{2,1,0:T(8,128)(2,1)} %broadcast_in_dim.2), calls=%async_computation.2 | async-start | bytes 1048576 | tf_op jit(solution)/shard_map/all_to_all | solution.py:217
where the time goes:
time: 136 us; the launch traced here: 135 us
  starting transfers between devices  53.8 us (40%)
  waiting for transfers between devices  37.8 us (28%)
  local copies, waits for them, and re-layouts  22.4 us (16%)
  Pallas kernels  14.7 us (11%)
  other arithmetic  5.28 us (4%)
    all_to_all x3, starting transfers between devices, exchange(): return lax.all_to_all(value, axes, split_axis=0, concat_axis=0, tiled=True)  36 us
    all_to_all x3, waiting for transfers between devices, exchange(): return lax.all_to_all(value, axes, split_axis=0, concat_axis=0, tiled=True)  30.4 us
    ppermute x6, starting transfers between devices, shifted(): return lax.ppermute(value, axes, pairs)  17.8 us
    pallas_call x1, Pallas kernels, on_device(): call(main_body, (jax.ShapeDtypeStruct((384, 512), BF), jax.ShapeDtypeStru...  10.7 us
    unnamed x27, local copies, waits for them, and re-layouts  9.46 us
    ppermute x6, waiting for transfers between devices, shifted(): return lax.ppermute(value, axes, pairs)  7.5 us
    reshape x1, local copies, waits for them, and re-layouts, on_device(): cot = cotangent.reshape(2, 384, 2048)  4.8 us
  transfers between devices with their start and end apart: 9, of which 5 were waited for; matrix products, arithmetic and copies ran while one was open for 12% of the time, Pallas kernels for 3%

commit v1 on v0

v1 whole, which is shorter than its diff:
```python
import math

import jax
import jax.numpy as jnp
from jax import lax
from jax.experimental import pallas as pl
from jax.experimental.pallas import tpu as pltpu
from jax.sharding import Mesh, PartitionSpec as P

BF = jnp.bfloat16
F32 = jnp.float32
BAND = ("xl", "z", "core")
PEERS = ("tm", "xl", "z", "core")
CHIPS = ("xl", "z", "tm")
NT = (((1,), (1,)), ((), ()))


def matmul(a, b):
    return jnp.dot(a, b, preferred_element_type=F32)


def matmul_nt(a, b):
    return lax.dot_general(a, b, NT, preferred_element_type=F32)


def call(body, outs, cost, scratch=(), grid=None, in_specs=None, out_specs=None, vmem=16):
    params = {}
    if grid is not None:
        params = {"grid": grid, "in_specs": in_specs, "out_specs": out_specs}
    elif in_specs is not None:
        params = {"in_specs": in_specs}
    return pl.pallas_call(
        body,
        out_shape=outs,
        scratch_shapes=list(scratch),
        cost_estimate=pl.CostEstimate(flops=int(cost[0]), bytes_accessed=int(cost[1]), transcendentals=0),
        compiler_params=pltpu.CompilerParams(vmem_limit_bytes=vmem * 1024 * 1024),
        **params,
    )


def ones_where(cond):
    return jnp.where(cond, 1.0, 0.0).astype(BF)


def select_body(me_ref, order_hbm, wt_hbm, send_ref, take_ref, wide_ref, order_ref, wt_ref, tall, sems):
    copies = [pltpu.make_async_copy(order_hbm, order_ref, sems.at[0]), pltpu.make_async_copy(wt_hbm, wt_ref, sems.at[1])]
    copies[0].start()
    copies[1].start()
    copies[0].wait()
    me = me_ref[0]
    order = order_ref[...]
    mine = ((order >> 14) * 32 + ((order >> 7) & 31)) == me
    local_id = (((order >> 12) & 3) * 2 + ((order >> 6) & 1)) * 64 + (order & 63)
    hits = ones_where(mine)
    up = lax.broadcasted_iota(jnp.int32, (128, 128), 0)
    lane = lax.broadcasted_iota(jnp.int32, (128, 128), 1)
    running = matmul(hits, ones_where(up <= lane))
    row = lax.broadcasted_iota(jnp.int32, (512, 512), 0)
    col = lax.broadcasted_iota(jnp.int32, (512, 512), 1)
    group = (row >> 2) == (col >> 2)
    above = matmul(ones_where(group & (col < row)), hits)
    running = running + jnp.sum(above, axis=1, keepdims=True)
    lane = lax.broadcasted_iota(jnp.int32, (512, 128), 1)
    slot = lax.broadcasted_iota(jnp.int32, (512, 128), 0) & 3
    found = jnp.zeros((512, 128), F32)
    for s in range(4):
        hit = mine & (running == s + 1.0)
        high = jnp.sum(jnp.where(hit, local_id >> 4, 0).astype(F32), axis=1, keepdims=True)
        low = jnp.sum(jnp.where(hit, local_id & 15, 0).astype(F32), axis=1, keepdims=True)
        found = found + jnp.where(lane == s, high, 0.0) + jnp.where(lane == s + 4, low, 0.0)
    found = matmul(ones_where(group), found.astype(BF))
    found = jnp.where(lane == slot, found * 16.0, 0.0) + jnp.where(lane == slot + 4, found, 0.0)
    place = 2 * jnp.sum(found, axis=1, keepdims=True).astype(jnp.int32)
    send_ref[...] = jnp.broadcast_to(place, (512, 128))
    pair = order_ref[pl.ds(pl.multiple_of((me >> 1) * 8, 8), 8), :]
    four = jnp.where((me & 1) == 0, pair[0:4], pair[4:8])
    own = jnp.concatenate([four[i : i + 1] for i in range(4)], axis=1)
    sender = (own >> 14) * 32 + ((own >> 7) & 31)
    pos = lax.broadcasted_iota(jnp.int32, (256, 512), 1)
    half = lax.broadcasted_iota(jnp.int32, (256, 512), 0)
    for e in range(2):
        here = pos == 2 * half + e
        mate = jnp.sum(jnp.where(here, sender, 0).astype(F32), axis=1, keepdims=True).astype(jnp.int32)
        earlier = (sender == mate) & (pos < 2 * half + e)
        count = jnp.sum(jnp.where(earlier, 1.0, 0.0), axis=1, keepdims=True)
        far = jnp.where((mate & 1) == (me & 1), 0, 256)
        take_ref[e] = jnp.broadcast_to(far + (mate >> 1) * 4 + count.astype(jnp.int32), (256, 128))
    copies[1].wait()
    tall[0:432, :] = wt_ref[...].astype(F32)
    tall[432:512, :] = jnp.zeros((80, 384), F32)
    wide_ref[...] = tall[...].T.astype(BF)


def main_body(
    tm_ref, core_ref, seg_ref, prev_hbm, lat_hbm, near_hbm, far_hbm, cot_hbm, wide_hbm, wt_hbm,
    keep_hbm, pair_hbm, own_hbm, gfar_hbm, gprev_hbm,
    prev, lat, near, far, cot, wide, wt, ext, patch0, patch1, pre0, pre1, total, spread,
    keep, pair, own, gfar, gprev, edges, sems, cot_sems, out_sems,
):
    lanes = lax.broadcasted_iota(jnp.int32, (1, 128), 1)
    near_row = 5 - 5 * core_ref[0]
    ins = [(prev_hbm, prev), (lat_hbm, lat), (near_hbm, near), (far_hbm, far), (wide_hbm, wide), (wt_hbm, wt)]
    ins = [pltpu.make_async_copy(src, dst, sems.at[i]) for i, (src, dst) in enumerate(ins)]
    for copy in ins:
        copy.start()

    def cot_copy(i):
        return pltpu.make_async_copy(cot_hbm.at[i >> 2, :, i & 3], cot.at[i], cot_sems.at[i])

    for i in range(8):
        cot_copy(i).start()
    patch0[432:512, :] = jnp.zeros((80, 512), BF)
    patch1[432:512, :] = jnp.zeros((80, 512), BF)
    total[...] = jnp.zeros_like(total)
    spread[...] = jnp.zeros_like(spread)
    for copy in ins[:4]:
        copy.wait()
    for b in range(2):
        for h in range(4):
            ext[b, 1, 0:2, 1 + h] = prev[h, b]
            ext[b, 1, 2:6, 1 + h] = lat[h, b]
        ext[b, 1, :, near_row] = near[b]
        ext[b, 1, :, 5 - near_row] = far[b]
        for fr in range(6):
            x = ext[b, 1, fr].astype(F32).reshape(96, 128)
            left = jnp.where(lanes == 0, 0.0, pltpu.roll(x, 1, 1))
            right = jnp.where(lanes == 127, 0.0, pltpu.roll(x, 127, 1))
            ext[b, 0, fr] = left.astype(BF).reshape(6, 16, 128)
            ext[b, 2, fr] = right.astype(BF).reshape(6, 16, 128)

    def factors(i):
        b = i >> 2
        frame = tm_ref[0] * 4 + (i & 3)
        seg = seg_ref[b, frame]
        result = []
        for a in range(3):
            before = frame - (2 - a)
            same = (before >= 0) & (seg_ref[b, jnp.maximum(before, 0)] == seg)
            result.append(jnp.where(same, 1.0, 0.0))
        return result

    def forward(i, patch, pre):
        b, f = i >> 2, i & 3
        masks = factors(i)
        for a in range(3):
            mask = jnp.full((16, 128), masks[a], F32).astype(BF)
            for r in range(3):
                for c in range(3):
                    top = (a * 9 + r * 3 + c) * 16
                    for h in range(4):
                        patch[top : top + 16, h * 128 : h * 128 + 128] = ext[b, c, f + a, h + r] * mask
        pre[...] = matmul(wide[...], patch[...])

    def backward(i, patch, pre):
        b, f = i >> 2, i & 3
        masks = factors(i)
        cot_copy(i).wait()
        cots = jnp.swapaxes(cot[i].astype(F32), 0, 1)
        grads = []
        for h in range(4):
            x = pre[:, h * 128 : h * 128 + 128]
            sig = 0.5 * jnp.tanh(0.5 * x) + 0.5
            grads.append((cots[h] * sig * (1.0 + x * (1.0 - sig))).astype(BF))
        grad = jnp.concatenate(grads, axis=1)
        total[...] += matmul_nt(patch[...], grad)
        back = matmul(wt[...], grad)
        for a in range(3):
            for c in range(3):
                for row in range(6):
                    acc = None
                    for r in range(3):
                        h = row - r
                        if 0 <= h < 4:
                            top = (a * 9 + r * 3 + c) * 16
                            term = back[top : top + 16, h * 128 : h * 128 + 128]
                            acc = term if acc is None else acc + term
                    spread[b, c, f + a, row] += acc * masks[a]

    for copy in ins[4:]:
        copy.wait()
    forward(0, patch0, pre0)

    def step(j, carry):
        i = 2 * j
        forward(i + 1, patch1, pre1)
        backward(i, patch0, pre0)
        forward(jnp.minimum(i + 2, 7), patch0, pre0)
        backward(i + 1, patch1, pre1)
        return carry

    lax.fori_loop(0, 4, step, 0)
    mine = core_ref[0] * 256
    for g in range(16):
        for i in range(3):
            cols = slice(i * 128, i * 128 + 128)
            kept = pl.multiple_of(mine + g * 16, 16)
            pair[g * 3 + i] = total[pl.ds(pl.multiple_of(256 - mine + g * 16, 16), 16), cols].astype(BF)
            keep[g * 3 + i] = total[pl.ds(kept, 16), cols].astype(BF)
    outs = [(pair, pair_hbm), (keep, keep_hbm), (gfar, gfar_hbm), (gprev, gprev_hbm), (own, own_hbm)]
    outs = [pltpu.make_async_copy(src, dst, out_sems.at[i]) for i, (src, dst) in enumerate(outs)]
    outs[1].start()
    for b in range(2):
        for fr in range(6):
            x0 = spread[b, 0, fr].reshape(96, 128)
            x2 = spread[b, 2, fr].reshape(96, 128)
            x = (
                spread[b, 1, fr].reshape(96, 128)
                + jnp.where(lanes == 127, 0.0, pltpu.roll(x0, 127, 1))
                + jnp.where(lanes == 0, 0.0, pltpu.roll(x2, 1, 1))
            ).reshape(6, 16, 128)
            edges[0] = x[0]
            edges[5] = x[5]
            pair[48 + b * 6 + fr] = edges[near_row].astype(BF)
            gfar[b, fr] = edges[5 - near_row].astype(BF)
            if fr < 2:
                gprev[b, fr] = x[1:5]
            else:
                own[b, fr - 2] = x[1:5]
    outs[0].start()
    for copy in outs[2:]:
        copy.start()
    for copy in outs:
        copy.wait()


def add_body(keep_ref, given_ref, out_ref):
    for g in range(16):
        for i in range(3):
            x = keep_ref[g * 3 + i].astype(F32) + given_ref[g * 3 + i].astype(F32)
            out_ref[g * 4 : g * 4 + 4, :, i * 128 : i * 128 + 128] = x.reshape(4, 4, 128).astype(BF)


def early_body(core_ref, gprev_ref, given_ref, far_ref, out_ref):
    near_row = 3 - 3 * core_ref[0]
    out_ref[...] = gprev_ref[...].astype(BF)
    for b in range(2):
        for f in range(2):
            near = given_ref[48 + b * 6 + f].astype(F32)
            out_ref[b, f, near_row] = (gprev_ref[b, f, near_row] + near).astype(BF)
            far = far_ref[b, f].astype(F32)
            out_ref[b, f, 3 - near_row] = (gprev_ref[b, f, 3 - near_row] + far).astype(BF)


def out_body(core_ref, own_ref, given_ref, far_ref, next_ref, send_ref, part_ref, twin_ref, out_ref, rows, grad):
    near_row = 3 - 3 * core_ref[0]
    grad[...] = own_ref[...]
    for b in range(2):
        for f in range(4):
            grad[b, f, near_row] += given_ref[50 + b * 6 + f].astype(F32)
            grad[b, f, 3 - near_row] += far_ref[b, 2 + f].astype(F32)
            for h in range(4):
                x = grad[b, f, h]
                if f >= 2:
                    x = x + next_ref[b, f - 2, h].astype(F32)
                x = x.astype(BF)
                top = (b * 2 + h % 2) * 16
                col = (f * 2 + h // 2) * 128
                rows[top : top + 16, col : col + 128] = x
                rows[64 + top : 80 + top, col : col + 128] = pltpu.roll(x.astype(F32), 127, 1).astype(BF)
    place = send_ref[...]
    lane = lax.broadcasted_iota(jnp.int32, (512, 128), 1)
    send = jnp.concatenate([ones_where(place == lane + i * 128) for i in range(8)], axis=1)
    tokens = matmul_nt(send, rows[...]).reshape(64, 2, 4, 128)
    out_ref[:, 0:2] = tokens.astype(BF)
    part = (part_ref[...] + twin_ref[...]) * (1.0 / math.sqrt(4 * 16 * 128 * 128))
    for i in range(3):
        piece = part[:, i * 128 : i * 128 + 128].astype(BF)
        out_ref[:, 2 + i] = jnp.broadcast_to(piece[None], (64, 4, 128))


def take_body(core_ref, mine_ref, other_ref, take_ref, out_ref, wg_ref):
    core = core_ref[0]
    got = jnp.concatenate([ref[:, core].astype(F32).reshape(256, 128) for ref in (mine_ref, other_ref)]).astype(BF)
    src = lax.broadcasted_iota(jnp.int32, (128, 128), 0)
    dst = lax.broadcasted_iota(jnp.int32, (128, 128), 1)
    lane = lax.broadcasted_iota(jnp.int32, (256, 128), 1)
    want = ((dst & 1) << 6) + (((dst >> 1) & 1) << 4) + ((dst >> 2) & 15)
    takes = []
    for e in range(2):
        row = take_ref[e]
        takes.append(jnp.concatenate([ones_where(row == lane + i * 128) for i in range(4)], axis=1))
    for b in range(2):
        total = None
        for e in range(2):
            place = ones_where((src == want + b * 32) & ((dst >> 6) == e))
            moved = matmul(got, place).astype(BF)
            term = matmul(takes[e], moved)
            total = term if total is None else total + term
        out_ref[b] = total.astype(BF)
    for i in range(3):
        mine = mine_ref[:, 2 + i].astype(F32)
        other = other_ref[:, 2 + i].astype(F32)
        halves = (jnp.where(core == 0, mine, other), jnp.where(core == 0, other, mine))
        for c in range(2):
            for j in range(64):
                top = c * 256 + (j & 15) * 16 + (j >> 4) * 4
                if top < 432:
                    wg_ref[top : top + 4, i * 128 : i * 128 + 128] = halves[c][j]


def shifted(value, step):
    count = lax.axis_size("tm")
    return lax.ppermute(value, "tm", [(i, i + step) for i in range(count) if 0 <= i + step < count])


def crossed(value):
    count = math.prod(lax.axis_size(a) for a in BAND)
    pairs = [(i, i + 1) for i in range(1, count - 1, 2)]
    return lax.ppermute(value, BAND, pairs + [(j, i) for i, j in pairs])


def swapped(value):
    return lax.ppermute(value, "core", [(0, 1), (1, 0)])


def exchange(value, axes):
    return lax.all_to_all(value, axes, split_axis=0, concat_axis=0, tiled=True)


def whole(shape):
    return pl.BlockSpec(shape, lambda b, f: (0,) * len(shape))


def on_device(latent, weight, cotangent, groups, order):
    tm = lax.axis_index("tm")
    core = lax.axis_index("core")
    me = tm * 32 + lax.axis_index(BAND)
    smem = pl.BlockSpec(memory_space=pltpu.SMEM)
    vmem = pl.BlockSpec(memory_space=pltpu.VMEM)
    hbm = pl.BlockSpec(memory_space=pltpu.HBM)
    tall = weight.T
    lat = latent.transpose(3, 0, 2, 1, 4)
    prev = shifted(lat[:, :, 2:4], 1)
    send, take, wide = call(
        select_body,
        (
            jax.ShapeDtypeStruct((512, 128), jnp.int32),
            jax.ShapeDtypeStruct((2, 256, 128), jnp.int32),
            jax.ShapeDtypeStruct((384, 512), BF),
        ),
        (500e6, 2e6),
        scratch=[
            pltpu.VMEM((512, 128), jnp.int32),
            pltpu.VMEM((432, 384), BF),
            pltpu.VMEM((512, 384), F32),
            pltpu.SemaphoreType.DMA((2,)),
        ],
        in_specs=[smem, hbm, hbm],
        vmem=60,
    )(me.reshape(1), order.reshape(512, 128), tall)
    prev, wide = lax.optimization_barrier((prev, wide))
    edge = lambda row: jnp.concatenate([lax.dynamic_index_in_dim(x, row, 0, False) for x in (prev, lat)], axis=1)
    far = crossed(edge(3 * core))
    near = swapped(edge(3 - 3 * core))
    outs = [
        ((48, 16, 128), BF),
        ((60, 16, 128), BF),
        ((2, 4, 4, 16, 128), F32),
        ((2, 6, 16, 128), BF),
        ((2, 2, 4, 16, 128), F32),
    ]
    keep, pair, grad, gfar, gprev = call(
        main_body,
        tuple(jax.ShapeDtypeStruct(*out) for out in outs),
        (4.5e9, 5e6),
        scratch=[
            pltpu.VMEM((4, 2, 2, 16, 128), BF),
            pltpu.VMEM((4, 2, 4, 16, 128), BF),
            pltpu.VMEM((2, 6, 16, 128), BF),
            pltpu.VMEM((2, 6, 16, 128), BF),
            pltpu.VMEM((8, 384, 4, 128), BF),
            pltpu.VMEM((384, 512), BF),
            pltpu.VMEM((432, 384), BF),
            pltpu.VMEM((2, 3, 6, 6, 16, 128), BF),
            pltpu.VMEM((512, 512), BF),
            pltpu.VMEM((512, 512), BF),
            pltpu.VMEM((384, 512), F32),
            pltpu.VMEM((384, 512), F32),
            pltpu.VMEM((512, 384), F32),
            pltpu.VMEM((2, 3, 6, 6, 16, 128), F32),
        ]
        + [pltpu.VMEM(*out) for out in outs]
        + [pltpu.VMEM((6, 16, 128), F32)]
        + [pltpu.SemaphoreType.DMA((n,)) for n in (6, 8, 5)],
        in_specs=[smem] * 3 + [hbm] * 7,
        out_specs=[hbm] * 5,
        vmem=60,
    )(tm.reshape(1), core.reshape(1), groups, prev, lat, near, far, cotangent, wide, tall)
    given = swapped(pair)
    half = call(add_body, jax.ShapeDtypeStruct((64, 4, 384), BF), (1e5, 6e5), in_specs=[vmem] * 2)(keep, given)
    from_far = crossed(gfar)
    early = call(
        early_body,
        jax.ShapeDtypeStruct((2, 2, 4, 16, 128), BF),
        (1e5, 3e5),
        in_specs=[smem] + [vmem] * 3,
    )(core.reshape(1), gprev, given, from_far)
    from_next = shifted(early, -1)
    parts = exchange(half, CHIPS)
    part = jnp.sum(parts.astype(F32), axis=0)
    twin = lax.ppermute(part, "rep", [(0, 1), (1, 0)])
    outgoing = call(
        out_body,
        jax.ShapeDtypeStruct((64, 5, 4, 128), BF),
        (150e6, 2e6),
        scratch=[pltpu.VMEM((128, 1024), BF), pltpu.VMEM((2, 4, 4, 16, 128), F32)],
        in_specs=[smem] + [vmem] * 7,
    )(core.reshape(1), grad, given, from_far, from_next, send, part, twin)
    got = exchange(outgoing, ("tm", "xl", "z"))
    other = swapped(got)
    tokens, summed = call(
        take_body,
        (jax.ShapeDtypeStruct((2, 256, 128), BF), jax.ShapeDtypeStruct((432, 384), F32)),
        (200e6, 1e6),
        in_specs=[smem] + [vmem] * 3,
    )(core.reshape(1), got, other, take)
    return tokens, summed.T


def solution(mesh):
    split = Mesh(mesh.devices.reshape(4, 2, 8, 2, 2), ("tm", "xl", "z", "core", "rep"))
    placed = P("rep", None, "tm", BAND, None)
    return jax.shard_map(
        on_device,
        mesh=split,
        in_specs=(placed, P(), placed, P("rep", None), P()),
        out_specs=(P("rep", PEERS, None), P()),
        check_vma=False,
    )
```

time: 136 us -> 95.3 us (0.70)
  waiting for transfers between devices: 37.8 us -> 10.9 us
  blocking collectives: 0 us -> 20.9 us
  starting transfers between devices: 53.8 us -> 34.2 us
  local copies, waits for them, and re-layouts: 22.4 us -> 4.38 us
  Pallas kernels: 14.7 us -> 23.5 us
  other arithmetic: 5.28 us -> 0.13 us
    all_to_all x3 -> x1, waiting for transfers between devices: 30.4 us -> 1.38 us  [exchange(): return lax.all_to_all(value, axes, split_axis=0, concat_axis=0, tiled=True)]
    all_to_all x3 -> x1, starting transfers between devices: 36 us -> 13.3 us  [exchange(): return lax.all_to_all(value, axes, split_axis=0, concat_axis=0, tiled=True)]
    all_to_all x0 -> x1, blocking collectives: none -> 20.9 us  [exchange(): return lax.all_to_all(value, axes, split_axis=0, concat_axis=0, tiled=True)]
    pallas_call x4 -> x6, Pallas kernels: 14.7 us -> 23.5 us  [the longest x1 16.8 us: on_device(): call(main_body, tuple((jax.ShapeDtypeStruct(*out) for out in outs)), (450...]
    reshape x5 -> x0, local copies, waits for them, and re-layouts: 7.41 us -> none  [the longest x1 4.8 us: on_device(): cot = cotangent.reshape(2, 384, 2048)]
    unnamed x27 -> x19, local copies, waits for them, and re-layouts: 9.46 us -> 4.35 us
    ppermute x6 -> x8, starting transfers between devices: 17.8 us -> 20.8 us  [the longest x2 7.19 us: crossed(): return lax.ppermute(value, BAND, pairs + [(j, i) for i, j in pairs])]
    scatter-add x2 -> x0, other arithmetic: 2.76 us -> none  [the longest x1 1.38 us: on_device(): early = gprev.at[:, :, 0].add(from_low[:, 0:2].astype(F32))]
  transfers between devices with their start and end apart: 9 -> 9, of which waited for: 5 -> 6; matrix products, arithmetic and copies ran while one was open for 12% -> 0% of each run, Pallas kernels for 3% -> 4%
where the time goes in v1:
time: 95.3 us; the launch traced here: 94.8 us
  starting transfers between devices  34.2 us (36%)
  Pallas kernels  23.5 us (25%)
  blocking collectives  20.9 us (22%)
  waiting for transfers between devices  10.9 us (11%)
  local copies, waits for them, and re-layouts  4.38 us (5%)
    all_to_all x1, blocking collectives, exchange(): return lax.all_to_all(value, axes, split_axis=0, concat_axis=0, tiled=True)  20.9 us
    pallas_call x1, Pallas kernels, on_device(): call(main_body, tuple((jax.ShapeDtypeStruct(*out) for out in outs)), (450...  16.8 us
    all_to_all x1, starting transfers between devices, exchange(): return lax.all_to_all(value, axes, split_axis=0, concat_axis=0, tiled=True)  13.3 us
    ppermute x2, starting transfers between devices, crossed(): return lax.ppermute(value, BAND, pairs + [(j, i) for i, j in pairs])  7.19 us
    ppermute x3, starting transfers between devices, swapped(): return lax.ppermute(value, 'core', [(0, 1), (1, 0)])  5.78 us
    ppermute x2, starting transfers between devices, shifted(): lax.ppermute(value, 'tm', [(i, i + step) for i in range(count) if 0 <= i...  5.33 us
    ppermute x2, waiting for transfers between devices, crossed(): return lax.ppermute(value, BAND, pairs + [(j, i) for i, j in pairs])  5.01 us
    unnamed x19, local copies, waits for them, and re-layouts  4.35 us
  transfers between devices with their start and end apart: 9, of which 6 were waited for; matrix products, arithmetic and copies ran while one was open for 0% of the time, Pallas kernels for 4%

profile of v1, /device:TPU:1, one launch (start us, length us, event | category | flops | bytes accessed | tf_op | source)
XLA Modules:
  0.0 94.8 jit_solution(10607936681304213461)
XLA Ops:
  0.6 0.9 copy.12
  1.6 0.0 copy-start.5
  1.6 4.0 %collective-permute-start = (bf16[4,2,2,16,128]{4,3,2,1,0:T(8,128)(2,1)S(1)}, bf16[4,2,2,16,128]{4,3,2,1,0:T(8,128)(2,1)S(1)}, u32[]{:S(2)}, u32[]{:S(2)}) collective-permute-start(bf16[4,2,2,16,128]{4,3,2,1,0:T(8,128)(2,1)S(1)} %slice.4), channel_id=1, source_target_pairs={{0,64},{64,128},{128,192},{1,65},{65,129},{129,193},{2,66},{66,130... | collective-permute-start | bytes 196616 | tf_op jit(solution)/shard_map/ppermute | solution.py:304
  5.7 3.5 %shard_map.68 = (s32[512,128]{1,0:T(8,128)}, s32[2,256,128]{2,1,0:T(8,128)}, bf16[384,512]{1,0:T(8,128)(2,1)}) custom-call(s32[1]{0:T(128)} %bitcast.3.me_ref, s32[512,128]{1,0:T(8,128)} %bitcast.25, bf16[432,384]{1,0:T(8,128)(2,1)} %bitcast.23), custom_call_target="tpu_custom_call" | custom-call | flops 500000000 | bytes 2000000 | tf_op jit(solution)/shard_map/pallas_call | solution.py:335
  9.2 0.0 collective-permute-done.prev_hbm
  9.2 0.0 copy-start.6
  9.3 1.0 %collective-permute-start.1 = (bf16[2,6,16,128]{3,2,1,0:T(8,128)(2,1)S(1)}, bf16[2,6,16,128]{3,2,1,0:T(8,128)(2,1)S(1)}, u32[]{:S(2)}, u32[]{:S(2)}) collective-permute-start(bf16[2,6,16,128]{3,2,1,0:T(8,128)(2,1)S(1)} %pad_maximum_fusion), channel_id=1, source_target_pairs={{0,2},{2,0},{1,3},{3,1},{4,6},{6,4},{5,7},{7,5},{8,10},{10,8},{9,1... | collective-permute-start | bytes 147464 | tf_op jit(solution)/shard_map/ppermute | solution.py:314
  10.3 3.5 %collective-permute-start.2 = (bf16[2,6,16,128]{3,2,1,0:T(8,128)(2,1)S(1)}, bf16[2,6,16,128]{3,2,1,0:T(8,128)(2,1)S(1)}, u32[]{:S(2)}, u32[]{:S(2)}) collective-permute-start(bf16[2,6,16,128]{3,2,1,0:T(8,128)(2,1)S(1)} %pad_maximum_fusion.1), channel_id=1, source_target_pairs={{2,4},{6,8},{10,12},{14,16},{18,20},{22,24},{26,28},{30,32},{34,36... | collective-permute-start | bytes 147464 | tf_op jit(solution)/shard_map/ppermute | solution.py:310
  13.8 0.0 collective-permute-done.1.near_hbm
  13.8 0.0 copy-start.7
  13.8 1.9 %collective-permute-done.2.far_hbm = bf16[2,6,16,128]{3,2,1,0:T(8,128)(2,1)S(1)} collective-permute-done((bf16[2,6,16,128]{3,2,1,0:T(8,128)(2,1)S(1)}, bf16[2,6,16,128]{3,2,1,0:T(8,128)(2,1)S(1)}, u32[]{:S(2)}, u32[]{:S(2)}) %collective-permute-start.2) | collective-permute-done | bytes 49184 | tf_op jit(solution)/shard_map/ppermute | solution.py:310
  15.7 0.0 copy-start.8
  15.7 0.0 copy-done.5
  15.7 0.0 copy-done.6
  15.7 0.0 copy-done.7
  15.7 0.6 copy-done.8
  16.3 0.0 copy-start.1
  16.3 16.8 %shard_map.69 = (bf16[48,16,128]{2,1,0:T(8,128)(2,1)}, bf16[60,16,128]{2,1,0:T(8,128)(2,1)}, f32[2,4,4,16,128]{4,3,2,1,0:T(8,128)}, bf16[2,6,16,128]{3,2,1,0:T(8,128)(2,1)}, f32[2,2,4,16,128]{4,3,2,1,0:T(8,128)}) custom-call(s32[1]{0:T(128)} %bitcast.1.tm_ref, s32[1]{0:T(128)} %bitcast.core_ref, s32[2,16]{1,0:T(2,128)} %seg_ref.1, ...), custom_call_target="tpu_custom_call" | custom-call | flops 4499999744 | bytes 5000000 | tf_op jit(solution)/shard_map/pallas_call | solution.py:363
  33.1 0.0 copy-start
  33.1 0.1 collective-permute-start.3
  33.2 1.7 %collective-permute-done.3.given_ref = bf16[60,16,128]{2,1,0:T(8,128)(2,1)S(1)} collective-permute-done((bf16[60,16,128]{2,1,0:T(8,128)(2,1)}, bf16[60,16,128]{2,1,0:T(8,128)(2,1)S(1)}, u32[]{:S(2)}, u32[]{:S(2)}) %collective-permute-start.3) | collective-permute-done | bytes 245792 | tf_op jit(solution)/shard_map/ppermute | solution.py:314
  35.0 0.0 copy-start.3
  35.0 0.9 copy-done.3
  35.9 0.8 shard_map.71
  36.6 13.3 %all-to-all-start = ((bf16[64,4,384]{2,1,0:T(4,128)(2,1)}), bf16[64,4,384]{2,1,0:T(4,128)(2,1)S(1)}, u32[]{:S(2)}, u32[]{:S(2)}) async-start(bf16[64,4,384]{2,1,0:T(4,128)(2,1)} %shard_map.71), calls=%async_computation | async-start | bytes 393216 | tf_op jit(solution)/shard_map/all_to_all | solution.py:318
  50.0 3.7 %collective-permute-start.4 = (bf16[2,6,16,128]{3,2,1,0:T(8,128)(2,1)}, bf16[2,6,16,128]{3,2,1,0:T(8,128)(2,1)S(1)}, u32[]{:S(2)}, u32[]{:S(2)}) collective-permute-start(bf16[2,6,16,128]{3,2,1,0:T(8,128)(2,1)} %get-tuple-element.19), channel_id=1, source_target_pairs={{2,4},{6,8},{10,12},{14,16},{18,20},{22,24},{26,28},{30,32},{34,36... | collective-permute-start | bytes 147464 | tf_op jit(solution)/shard_map/ppermute | solution.py:310
  53.7 3.1 %collective-permute-done.4.far_ref = bf16[2,6,16,128]{3,2,1,0:T(8,128)(2,1)S(1)} collective-permute-done((bf16[2,6,16,128]{3,2,1,0:T(8,128)(2,1)}, bf16[2,6,16,128]{3,2,1,0:T(8,128)(2,1)S(1)}, u32[]{:S(2)}, u32[]{:S(2)}) %collective-permute-start.4) | collective-permute-done | bytes 49184 | tf_op jit(solution)/shard_map/ppermute | solution.py:310
  56.8 0.0 copy-start.4
  56.8 0.9 copy-done.4
  57.7 1.3 %collective-permute-start.5 = (bf16[2,2,4,16,128]{4,3,2,1,0:T(8,128)(2,1)S(1)}, bf16[2,2,4,16,128]{4,3,2,1,0:T(8,128)(2,1)S(1)}, u32[]{:S(2)}, u32[]{:S(2)}) collective-permute-start(bf16[2,2,4,16,128]{4,3,2,1,0:T(8,128)(2,1)S(1)} %shard_map.70), channel_id=1, source_target_pairs={{64,0},{128,64},{192,128},{65,1},{129,65},{193,129},{66,2},{130,66... | collective-permute-start | bytes 196616 | tf_op jit(solution)/shard_map/ppermute | solution.py:304
  59.0 1.4 %all-to-all-done = bf16[64,4,384]{2,1,0:T(4,128)(2,1)S(1)} async-done(((bf16[64,4,384]{2,1,0:T(4,128)(2,1)}), bf16[64,4,384]{2,1,0:T(4,128)(2,1)S(1)}, u32[]{:S(2)}, u32[]{:S(2)}) %all-to-all-start) | async-done | bytes 196640 | tf_op jit(solution)/shard_map/all_to_all | solution.py:318
  60.4 0.1 convert_reduce_fusion.part_ref
  60.5 2.5 %collective-permute-start.6 = (f32[4,384]{1,0:T(4,128)S(1)}, f32[4,384]{1,0:T(4,128)S(1)}, u32[]{:S(2)}, u32[]{:S(2)}) collective-permute-start(f32[4,384]{1,0:T(4,128)S(1)} %convert_reduce_fusion.part_ref), channel_id=1, source_target_pairs={{0,1},{1,0},{2,3},{3,2},{4,5},{5,4},{6,7},{7,6},{8,9},{9,8},{10,11... | collective-permute-start | bytes 18440 | tf_op jit(solution)/shard_map/ppermute | solution.py:402
  63.1 0.0 collective-permute-done.5.next_ref
  63.1 1.5 %collective-permute-done.6.twin_ref = f32[4,384]{1,0:T(4,128)S(1)} collective-permute-done((f32[4,384]{1,0:T(4,128)S(1)}, f32[4,384]{1,0:T(4,128)S(1)}, u32[]{:S(2)}, u32[]{:S(2)}) %collective-permute-start.6) | collective-permute-done | bytes 6176 | tf_op jit(solution)/shard_map/ppermute | solution.py:402
  64.6 0.0 copy-done.1
  64.6 0.0 copy-start.2
  64.6 0.9 %copy-done.2 = f32[2,4,4,16,128]{4,3,2,1,0:T(8,128)S(1)} copy-done((f32[2,4,4,16,128]{4,3,2,1,0:T(8,128)S(1)}, f32[2,4,4,16,128]{4,3,2,1,0:T(8,128)}, u32[]{:S(2)}) %copy-start.2) | copy-done | bytes 262168
  65.6 0.6 shard_map.72
  66.2 20.9 %all_to_all.10.mine_ref = bf16[64,5,4,128]{3,2,1,0:T(4,128)(2,1)S(1)} all-to-all(bf16[64,5,4,128]{3,2,1,0:T(4,128)(2,1)S(1)} %shard_map.72), channel_id=1, replica_groups=mesh['tm'=4,'xl'=2,'z'=8,'core'=2,'rep'=2] {'tm','xl','z'}, dimensions={0} | all-to-all | bytes 655360 | tf_op jit(solution)/shard_map/all_to_all | solution.py:318
  87.1 4.6 %collective-permute-start.7 = (bf16[64,5,4,128]{3,2,1,0:T(4,128)(2,1)S(1)}, bf16[64,5,4,128]{3,2,1,0:T(4,128)(2,1)S(1)}, u32[]{:S(2)}, u32[]{:S(2)}) collective-permute-start(bf16[64,5,4,128]{3,2,1,0:T(4,128)(2,1)S(1)} %all_to_all.10.mine_ref), channel_id=1, source_target_pairs={{0,2},{2,0},{1,3},{3,1},{4,6},{6,4},{5,7},{7,5},{8,10},{10,8},{9,1... | collective-permute-start | bytes 983048 | tf_op jit(solution)/shard_map/ppermute | solution.py:314
  91.7 1.3 %collective-permute-done.7.other_ref = bf16[64,5,4,128]{3,2,1,0:T(4,128)(2,1)S(1)} collective-permute-done((bf16[64,5,4,128]{3,2,1,0:T(4,128)(2,1)S(1)}, bf16[64,5,4,128]{3,2,1,0:T(4,128)(2,1)S(1)}, u32[]{:S(2)}, u32[]{:S(2)}) %collective-permute-start.7) | collective-permute-done | bytes 327712 | tf_op jit(solution)/shard_map/ppermute | solution.py:314
  93.0 0.0 copy-done
  93.0 1.9 %shard_map.73 = (bf16[2,256,128]{2,1,0:T(8,128)(2,1)}, f32[432,384]{1,0:T(8,128)}) custom-call(s32[1]{0:T(128)} %bitcast.core_ref, bf16[64,5,4,128]{3,2,1,0:T(4,128)(2,1)S(1)} %all_to_all.10.mine_ref, bf16[64,5,4,128]{3,2,1,0:T(4,128)(2,1)S(1)} %collective-permute-done.7.other_ref, s32[2,256,128]{2,1,0:T(8,128)S(1)} %copy-done), custom_call_target="tpu_custom_call" | custom-call | flops 200000000 | bytes 1000000 | tf_op jit(solution)/shard_map/pallas_call | solution.py:412
  (6 shorter events, 0.1 us)
Async XLA Ops:
  1.6 14.1 %copy-start.5 = (bf16[2,16,4,4,128]{4,1,2,0,3:T(8,128)(2,1)}, bf16[2,16,4,4,128]{4,1,2,0,3:T(8,128)(2,1)S(1)}, u32[]{:S(2)}) copy-start(bf16[2,16,4,4,128]{4,1,2,0,3:T(8,128)(2,1)S(1)} %copy.12) | copy-start | bytes 393220
  1.6 7.6 %collective-permute-start = (bf16[4,2,2,16,128]{4,3,2,1,0:T(8,128)(2,1)S(1)}, bf16[4,2,2,16,128]{4,3,2,1,0:T(8,128)(2,1)S(1)}, u32[]{:S(2)}, u32[]{:S(2)}) collective-permute-start(bf16[4,2,2,16,128]{4,3,2,1,0:T(8,128)(2,1)S(1)} %slice.4), channel_id=1, source_target_pairs={{0,64},{64,128},{128,192},{1,65},{65,129},{129,193},{2,66},{66,130... | collective-permute-start | bytes 196616 | tf_op jit(solution)/shard_map/ppermute | solution.py:304
  9.2 6.5 %copy-start.6 = (bf16[4,2,2,16,128]{4,3,2,1,0:T(8,128)(2,1)}, bf16[4,2,2,16,128]{4,3,2,1,0:T(8,128)(2,1)S(1)}, u32[]{:S(2)}) copy-start(bf16[4,2,2,16,128]{4,3,2,1,0:T(8,128)(2,1)S(1)} %collective-permute-done.prev_hbm) | copy-start | bytes 196612
  9.3 4.5 %collective-permute-start.1 = (bf16[2,6,16,128]{3,2,1,0:T(8,128)(2,1)S(1)}, bf16[2,6,16,128]{3,2,1,0:T(8,128)(2,1)S(1)}, u32[]{:S(2)}, u32[]{:S(2)}) collective-permute-start(bf16[2,6,16,128]{3,2,1,0:T(8,128)(2,1)S(1)} %pad_maximum_fusion), channel_id=1, source_target_pairs={{0,2},{2,0},{1,3},{3,1},{4,6},{6,4},{5,7},{7,5},{8,10},{10,8},{9,1... | collective-permute-start | bytes 147464 | tf_op jit(solution)/shard_map/ppermute | solution.py:314
  10.3 5.4 %collective-permute-start.2 = (bf16[2,6,16,128]{3,2,1,0:T(8,128)(2,1)S(1)}, bf16[2,6,16,128]{3,2,1,0:T(8,128)(2,1)S(1)}, u32[]{:S(2)}, u32[]{:S(2)}) collective-permute-start(bf16[2,6,16,128]{3,2,1,0:T(8,128)(2,1)S(1)} %pad_maximum_fusion.1), channel_id=1, source_target_pairs={{2,4},{6,8},{10,12},{14,16},{18,20},{22,24},{26,28},{30,32},{34,36... | collective-permute-start | bytes 147464 | tf_op jit(solution)/shard_map/ppermute | solution.py:310
  13.8 1.9 %copy-start.7 = (bf16[2,6,16,128]{3,2,1,0:T(8,128)(2,1)}, bf16[2,6,16,128]{3,2,1,0:T(8,128)(2,1)S(1)}, u32[]{:S(2)}) copy-start(bf16[2,6,16,128]{3,2,1,0:T(8,128)(2,1)S(1)} %collective-permute-done.1.near_hbm) | copy-start | bytes 147460
  15.7 0.6 copy-start.8
  16.3 48.3 %copy-start.1 = (s32[512,128]{1,0:T(8,128)S(1)}, s32[512,128]{1,0:T(8,128)}, u32[]{:S(2)}) copy-start(s32[512,128]{1,0:T(8,128)} %get-tuple-element.21.send_ref) | copy-start | bytes 786436
  33.1 59.8 %copy-start = (s32[2,256,128]{2,1,0:T(8,128)S(1)}, s32[2,256,128]{2,1,0:T(8,128)}, u32[]{:S(2)}) copy-start(s32[2,256,128]{2,1,0:T(8,128)} %get-tuple-element.23.take_ref) | copy-start | bytes 786436
  33.1 1.8 %collective-permute-start.3 = (bf16[60,16,128]{2,1,0:T(8,128)(2,1)}, bf16[60,16,128]{2,1,0:T(8,128)(2,1)S(1)}, u32[]{:S(2)}, u32[]{:S(2)}) collective-permute-start(bf16[60,16,128]{2,1,0:T(8,128)(2,1)} %get-tuple-element.18), channel_id=1, source_target_pairs={{0,2},{2,0},{1,3},{3,1},{4,6},{6,4},{5,7},{7,5},{8,10},{10,8},{9,1... | collective-permute-start | bytes 737288 | tf_op jit(solution)/shard_map/ppermute | solution.py:314
  35.0 0.9 copy-start.3
  36.6 23.8 %all-to-all-start = ((bf16[64,4,384]{2,1,0:T(4,128)(2,1)}), bf16[64,4,384]{2,1,0:T(4,128)(2,1)S(1)}, u32[]{:S(2)}, u32[]{:S(2)}) async-start(bf16[64,4,384]{2,1,0:T(4,128)(2,1)} %shard_map.71), calls=%async_computation | async-start | bytes 393216 | tf_op jit(solution)/shard_map/all_to_all | solution.py:318
  50.0 6.8 %collective-permute-start.4 = (bf16[2,6,16,128]{3,2,1,0:T(8,128)(2,1)}, bf16[2,6,16,128]{3,2,1,0:T(8,128)(2,1)S(1)}, u32[]{:S(2)}, u32[]{:S(2)}) collective-permute-start(bf16[2,6,16,128]{3,2,1,0:T(8,128)(2,1)} %get-tuple-element.19), channel_id=1, source_target_pairs={{2,4},{6,8},{10,12},{14,16},{18,20},{22,24},{26,28},{30,32},{34,36... | collective-permute-start | bytes 147464 | tf_op jit(solution)/shard_map/ppermute | solution.py:310
  56.8 0.9 copy-start.4
  57.7 5.3 %collective-permute-start.5 = (bf16[2,2,4,16,128]{4,3,2,1,0:T(8,128)(2,1)S(1)}, bf16[2,2,4,16,128]{4,3,2,1,0:T(8,128)(2,1)S(1)}, u32[]{:S(2)}, u32[]{:S(2)}) collective-permute-start(bf16[2,2,4,16,128]{4,3,2,1,0:T(8,128)(2,1)S(1)} %shard_map.70), channel_id=1, source_target_pairs={{64,0},{128,64},{192,128},{65,1},{129,65},{193,129},{66,2},{130,66... | collective-permute-start | bytes 196616 | tf_op jit(solution)/shard_map/ppermute | solution.py:304
  60.5 4.1 %collective-permute-start.6 = (f32[4,384]{1,0:T(4,128)S(1)}, f32[4,384]{1,0:T(4,128)S(1)}, u32[]{:S(2)}, u32[]{:S(2)}) collective-permute-start(f32[4,384]{1,0:T(4,128)S(1)} %convert_reduce_fusion.part_ref), channel_id=1, source_target_pairs={{0,1},{1,0},{2,3},{3,2},{4,5},{5,4},{6,7},{7,6},{8,9},{9,8},{10,11... | collective-permute-start | bytes 18440 | tf_op jit(solution)/shard_map/ppermute | solution.py:402
  64.6 1.0 %copy-start.2 = (f32[2,4,4,16,128]{4,3,2,1,0:T(8,128)S(1)}, f32[2,4,4,16,128]{4,3,2,1,0:T(8,128)}, u32[]{:S(2)}) copy-start(f32[2,4,4,16,128]{4,3,2,1,0:T(8,128)} %get-tuple-element.17.own_ref) | copy-start | bytes 786436
  87.1 5.9 %collective-permute-start.7 = (bf16[64,5,4,128]{3,2,1,0:T(4,128)(2,1)S(1)}, bf16[64,5,4,128]{3,2,1,0:T(4,128)(2,1)S(1)}, u32[]{:S(2)}, u32[]{:S(2)}) collective-permute-start(bf16[64,5,4,128]{3,2,1,0:T(4,128)(2,1)S(1)} %all_to_all.10.mine_ref), channel_id=1, source_target_pairs={{0,2},{2,0},{1,3},{3,1},{4,6},{6,4},{5,7},{7,5},{8,10},{10,8},{9,1... | collective-permute-start | bytes 983048 | tf_op jit(solution)/shard_map/ppermute | solution.py:314

commit v2 on v1

--- a/solution.py
+++ b/solution.py
@@ -23,12 +23,35 @@
     return lax.dot_general(a, b, NT, preferred_element_type=F32)
 
 
+MAIN_OUTS = [
+    ((48, 16, 128), BF),
+    ((60, 16, 128), BF),
+    ((2, 4, 4, 16, 128), F32),
+    ((2, 6, 16, 128), BF),
+    ((2, 2, 4, 16, 128), F32),
+]
+MAIN_SCRATCH = [
+    ((8, 384, 4, 128), BF),
+    ((2, 3, 6, 6, 16, 128), BF),
+    ((512, 512), BF),
+    ((384, 512), F32),
+    ((384, 512), F32),
+    ((2, 3, 6, 6, 16, 128), F32),
+    ((6, 16, 128), F32),
+    ((1536, 128), F32),
+    ((384, 512), BF),
+    ((512, 384), F32),
+]
+
+
 def call(body, outs, cost, scratch=(), grid=None, in_specs=None, out_specs=None, vmem=16):
     params = {}
     if grid is not None:
         params = {"grid": grid, "in_specs": in_specs, "out_specs": out_specs}
     elif in_specs is not None:
         params = {"in_specs": in_specs}
+        if out_specs is not None:
+            params["out_specs"] = out_specs
     return pl.pallas_call(
         body,
         out_shape=outs,
@@ -43,11 +66,22 @@
     return jnp.where(cond, 1.0, 0.0).astype(BF)
 
 
-def select_body(me_ref, order_hbm, wt_hbm, send_ref, take_ref, wide_ref, order_ref, wt_ref, tall, sems):
-    copies = [pltpu.make_async_copy(order_hbm, order_ref, sems.at[0]), pltpu.make_async_copy(wt_hbm, wt_ref, sems.at[1])]
-    copies[0].start()
-    copies[1].start()
-    copies[0].wait()
+def weight_body(me_ref, seg_ref, wt_ref, wide_ref, copy_ref, mask_ref, tall):
+    me = me_ref[0]
+    for b in range(2):
+        for f in range(4):
+            frame = (me >> 5) * 4 + f
+            for a in range(3):
+                before = frame - (2 - a)
+                same = (before >= 0) & (seg_ref[b, jnp.maximum(before, 0)] == seg_ref[b, frame])
+                mask_ref[12 * b + 3 * f + a] = jnp.where(same, 1, 0)
+    copy_ref[...] = wt_ref[...]
+    tall[0:432, :] = wt_ref[...].astype(F32)
+    tall[432:512, :] = jnp.zeros((80, 384), F32)
+    wide_ref[...] = (tall[...] * 0.5).T.astype(BF)
+
+
+def select_body(me_ref, order_ref, send_ref, take_ref):
     me = me_ref[0]
     order = order_ref[...]
     mine = ((order >> 14) * 32 + ((order >> 7) & 31)) == me
@@ -86,36 +120,23 @@
         count = jnp.sum(jnp.where(earlier, 1.0, 0.0), axis=1, keepdims=True)
         far = jnp.where((mate & 1) == (me & 1), 0, 256)
         take_ref[e] = jnp.broadcast_to(far + (mate >> 1) * 4 + count.astype(jnp.int32), (256, 128))
-    copies[1].wait()
-    tall[0:432, :] = wt_ref[...].astype(F32)
-    tall[432:512, :] = jnp.zeros((80, 384), F32)
-    wide_ref[...] = tall[...].T.astype(BF)
 
 
 def main_body(
-    tm_ref, core_ref, seg_ref, prev_hbm, lat_hbm, near_hbm, far_hbm, cot_hbm, wide_hbm, wt_hbm,
-    keep_hbm, pair_hbm, own_hbm, gfar_hbm, gprev_hbm,
-    prev, lat, near, far, cot, wide, wt, ext, patch0, patch1, pre0, pre1, total, spread,
-    keep, pair, own, gfar, gprev, edges, sems, cot_sems, out_sems,
+    core_ref, mask_ref, prev, lat, near, far, cot_hbm, wide, wt, keep, pair, own, gfar, gprev,
+    cot, ext, patch, pre, total, spread, edges, cots, grad, turned, cot_sems,
 ):
     lanes = lax.broadcasted_iota(jnp.int32, (1, 128), 1)
     near_row = 5 - 5 * core_ref[0]
-    ins = [(prev_hbm, prev), (lat_hbm, lat), (near_hbm, near), (far_hbm, far), (wide_hbm, wide), (wt_hbm, wt)]
-    ins = [pltpu.make_async_copy(src, dst, sems.at[i]) for i, (src, dst) in enumerate(ins)]
-    for copy in ins:
-        copy.start()
 
     def cot_copy(i):
         return pltpu.make_async_copy(cot_hbm.at[i >> 2, :, i & 3], cot.at[i], cot_sems.at[i])
 
     for i in range(8):
         cot_copy(i).start()
-    patch0[432:512, :] = jnp.zeros((80, 512), BF)
-    patch1[432:512, :] = jnp.zeros((80, 512), BF)
+    patch[432:512, :] = jnp.zeros((80, 512), BF)
     total[...] = jnp.zeros_like(total)
     spread[...] = jnp.zeros_like(spread)
-    for copy in ins[:4]:
-        copy.wait()
     for b in range(2):
         for h in range(4):
             ext[b, 1, 0:2, 1 + h] = prev[h, b]
@@ -130,17 +151,9 @@
             ext[b, 2, fr] = right.astype(BF).reshape(6, 16, 128)
 
     def factors(i):
-        b = i >> 2
-        frame = tm_ref[0] * 4 + (i & 3)
-        seg = seg_ref[b, frame]
-        result = []
-        for a in range(3):
-            before = frame - (2 - a)
-            same = (before >= 0) & (seg_ref[b, jnp.maximum(before, 0)] == seg)
-            result.append(jnp.where(same, 1.0, 0.0))
-        return result
-
-    def forward(i, patch, pre):
+        return [mask_ref[3 * i + a].astype(F32) for a in range(3)]
+
+    def build(i):
         b, f = i >> 2, i & 3
         masks = factors(i)
         for a in range(3):
@@ -150,56 +163,52 @@
                     top = (a * 9 + r * 3 + c) * 16
                     for h in range(4):
                         patch[top : top + 16, h * 128 : h * 128 + 128] = ext[b, c, f + a, h + r] * mask
+
+    def relayout(i):
+        cot_copy(i).wait()
+        cots[...] = cot[i].astype(F32).reshape(1536, 128)
+
+    def elements(h):
+        x = pre[:, h * 128 : h * 128 + 128]
+        t = jnp.tanh(x)
+        cot = cots[pl.ds(h, 384, stride=4), :]
+        grad[:, h * 128 : h * 128 + 128] = (cot * (1.0 + t) * (1.0 + x * (1.0 - t))).astype(BF)
+
+    def spread_tap(i, a, back):
+        b, f = i >> 2, i & 3
+        mask = factors(i)[a]
+        for c in range(3):
+            for row in range(6):
+                acc = None
+                for r in range(3):
+                    h = row - r
+                    if 0 <= h < 4:
+                        top = (r * 3 + c) * 16
+                        term = back[top : top + 16, h * 128 : h * 128 + 128]
+                        acc = term if acc is None else acc + term
+                spread[b, c, f + a, row] += acc * mask
+
+    def step(i, carry):
+        build(i)
+        relayout(i)
         pre[...] = matmul(wide[...], patch[...])
-
-    def backward(i, patch, pre):
-        b, f = i >> 2, i & 3
-        masks = factors(i)
-        cot_copy(i).wait()
-        cots = jnp.swapaxes(cot[i].astype(F32), 0, 1)
-        grads = []
         for h in range(4):
-            x = pre[:, h * 128 : h * 128 + 128]
-            sig = 0.5 * jnp.tanh(0.5 * x) + 0.5
-            grads.append((cots[h] * sig * (1.0 + x * (1.0 - sig))).astype(BF))
-        grad = jnp.concatenate(grads, axis=1)
-        total[...] += matmul_nt(patch[...], grad)
-        back = matmul(wt[...], grad)
+            elements(h)
+        back = matmul(wt[...], grad[...])
+        total[...] += matmul_nt(grad[...], patch[...])
         for a in range(3):
-            for c in range(3):
-                for row in range(6):
-                    acc = None
-                    for r in range(3):
-                        h = row - r
-                        if 0 <= h < 4:
-                            top = (a * 9 + r * 3 + c) * 16
-                            term = back[top : top + 16, h * 128 : h * 128 + 128]
-                            acc = term if acc is None else acc + term
-                    spread[b, c, f + a, row] += acc * masks[a]
-
-    for copy in ins[4:]:
-        copy.wait()
-    forward(0, patch0, pre0)
-
-    def step(j, carry):
-        i = 2 * j
-        forward(i + 1, patch1, pre1)
-        backward(i, patch0, pre0)
-        forward(jnp.minimum(i + 2, 7), patch0, pre0)
-        backward(i + 1, patch1, pre1)
+            spread_tap(i, a, back[a * 144 : a * 144 + 144])
         return carry
 
-    lax.fori_loop(0, 4, step, 0)
+    lax.fori_loop(0, 8, step, 0)
+    turned[...] = total[...].T
     mine = core_ref[0] * 256
     for g in range(16):
         for i in range(3):
             cols = slice(i * 128, i * 128 + 128)
             kept = pl.multiple_of(mine + g * 16, 16)
-            pair[g * 3 + i] = total[pl.ds(pl.multiple_of(256 - mine + g * 16, 16), 16), cols].astype(BF)
-            keep[g * 3 + i] = total[pl.ds(kept, 16), cols].astype(BF)
-    outs = [(pair, pair_hbm), (keep, keep_hbm), (gfar, gfar_hbm), (gprev, gprev_hbm), (own, own_hbm)]
-    outs = [pltpu.make_async_copy(src, dst, out_sems.at[i]) for i, (src, dst) in enumerate(outs)]
-    outs[1].start()
+            pair[g * 3 + i] = turned[pl.ds(pl.multiple_of(256 - mine + g * 16, 16), 16), cols].astype(BF)
+            keep[g * 3 + i] = turned[pl.ds(kept, 16), cols].astype(BF)
     for b in range(2):
         for fr in range(6):
             x0 = spread[b, 0, fr].reshape(96, 128)
@@ -208,7 +217,7 @@
                 spread[b, 1, fr].reshape(96, 128)
                 + jnp.where(lanes == 127, 0.0, pltpu.roll(x0, 127, 1))
                 + jnp.where(lanes == 0, 0.0, pltpu.roll(x2, 1, 1))
-            ).reshape(6, 16, 128)
+            ).reshape(6, 16, 128) * 0.5
             edges[0] = x[0]
             edges[5] = x[5]
             pair[48 + b * 6 + fr] = edges[near_row].astype(BF)
@@ -217,29 +226,21 @@
                 gprev[b, fr] = x[1:5]
             else:
                 own[b, fr - 2] = x[1:5]
-    outs[0].start()
-    for copy in outs[2:]:
-        copy.start()
-    for copy in outs:
-        copy.wait()
-
-
-def add_body(keep_ref, given_ref, out_ref):
+
+
+def mix_body(core_ref, keep_ref, given_ref, gprev_ref, far_ref, half_ref, early_ref):
     for g in range(16):
         for i in range(3):
             x = keep_ref[g * 3 + i].astype(F32) + given_ref[g * 3 + i].astype(F32)
-            out_ref[g * 4 : g * 4 + 4, :, i * 128 : i * 128 + 128] = x.reshape(4, 4, 128).astype(BF)
-
-
-def early_body(core_ref, gprev_ref, given_ref, far_ref, out_ref):
+            half_ref[g * 4 : g * 4 + 4, :, i * 128 : i * 128 + 128] = x.reshape(4, 4, 128).astype(BF)
     near_row = 3 - 3 * core_ref[0]
-    out_ref[...] = gprev_ref[...].astype(BF)
+    early_ref[...] = gprev_ref[...].astype(BF)
     for b in range(2):
         for f in range(2):
             near = given_ref[48 + b * 6 + f].astype(F32)
-            out_ref[b, f, near_row] = (gprev_ref[b, f, near_row] + near).astype(BF)
+            early_ref[b, f, near_row] = (gprev_ref[b, f, near_row] + near).astype(BF)
             far = far_ref[b, f].astype(F32)
-            out_ref[b, f, 3 - near_row] = (gprev_ref[b, f, 3 - near_row] + far).astype(BF)
+            early_ref[b, f, 3 - near_row] = (gprev_ref[b, f, 3 - near_row] + far).astype(BF)
 
 
 def out_body(core_ref, own_ref, given_ref, far_ref, next_ref, send_ref, part_ref, twin_ref, out_ref, rows, grad):
@@ -263,7 +264,7 @@
     send = jnp.concatenate([ones_where(place == lane + i * 128) for i in range(8)], axis=1)
     tokens = matmul_nt(send, rows[...]).reshape(64, 2, 4, 128)
     out_ref[:, 0:2] = tokens.astype(BF)
-    part = (part_ref[...] + twin_ref[...]) * (1.0 / math.sqrt(4 * 16 * 128 * 128))
+    part = (part_ref[...] + twin_ref[...]) * (0.5 / math.sqrt(4 * 16 * 128 * 128))
     for i in range(3):
         piece = part[:, i * 128 : i * 128 + 128].astype(BF)
         out_ref[:, 2 + i] = jnp.broadcast_to(piece[None], (64, 4, 128))
@@ -329,73 +330,51 @@
     smem = pl.BlockSpec(memory_space=pltpu.SMEM)
     vmem = pl.BlockSpec(memory_space=pltpu.VMEM)
     hbm = pl.BlockSpec(memory_space=pltpu.HBM)
-    tall = weight.T
     lat = latent.transpose(3, 0, 2, 1, 4)
     prev = shifted(lat[:, :, 2:4], 1)
-    send, take, wide = call(
-        select_body,
+    wide, tall, masks = call(
+        weight_body,
         (
-            jax.ShapeDtypeStruct((512, 128), jnp.int32),
-            jax.ShapeDtypeStruct((2, 256, 128), jnp.int32),
             jax.ShapeDtypeStruct((384, 512), BF),
+            jax.ShapeDtypeStruct((432, 384), BF),
+            jax.ShapeDtypeStruct((24,), jnp.int32),
         ),
-        (500e6, 2e6),
-        scratch=[
-            pltpu.VMEM((512, 128), jnp.int32),
-            pltpu.VMEM((432, 384), BF),
-            pltpu.VMEM((512, 384), F32),
-            pltpu.SemaphoreType.DMA((2,)),
-        ],
-        in_specs=[smem, hbm, hbm],
-        vmem=60,
-    )(me.reshape(1), order.reshape(512, 128), tall)
-    prev, wide = lax.optimization_barrier((prev, wide))
+        (1e6, 2e6),
+        scratch=[pltpu.VMEM((512, 384), F32)],
+        in_specs=[smem, smem, vmem],
+        out_specs=[vmem] * 2 + [smem],
+        vmem=52,
+    )(me.reshape(1), groups, weight.T)
+    prev, masks = lax.optimization_barrier((prev, masks))
     edge = lambda row: jnp.concatenate([lax.dynamic_index_in_dim(x, row, 0, False) for x in (prev, lat)], axis=1)
     far = crossed(edge(3 * core))
     near = swapped(edge(3 - 3 * core))
-    outs = [
-        ((48, 16, 128), BF),
-        ((60, 16, 128), BF),
-        ((2, 4, 4, 16, 128), F32),
-        ((2, 6, 16, 128), BF),
-        ((2, 2, 4, 16, 128), F32),
-    ]
+    send, take = call(
+        select_body,
+        (jax.ShapeDtypeStruct((512, 128), jnp.int32), jax.ShapeDtypeStruct((2, 256, 128), jnp.int32)),
+        (500e6, 2e6),
+        in_specs=[smem, vmem],
+        out_specs=[vmem] * 2,
+        vmem=52,
+    )(me.reshape(1), order.reshape(512, 128))
+    far, send = lax.optimization_barrier((far, send))
     keep, pair, grad, gfar, gprev = call(
         main_body,
-        tuple(jax.ShapeDtypeStruct(*out) for out in outs),
+        tuple(jax.ShapeDtypeStruct(*out) for out in MAIN_OUTS),
         (4.5e9, 5e6),
-        scratch=[
-            pltpu.VMEM((4, 2, 2, 16, 128), BF),
-            pltpu.VMEM((4, 2, 4, 16, 128), BF),
-            pltpu.VMEM((2, 6, 16, 128), BF),
-            pltpu.VMEM((2, 6, 16, 128), BF),
-            pltpu.VMEM((8, 384, 4, 128), BF),
-            pltpu.VMEM((384, 512), BF),
-            pltpu.VMEM((432, 384), BF),
-            pltpu.VMEM((2, 3, 6, 6, 16, 128), BF),
-            pltpu.VMEM((512, 512), BF),
-            pltpu.VMEM((512, 512), BF),
-            pltpu.VMEM((384, 512), F32),
-            pltpu.VMEM((384, 512), F32),
-            pltpu.VMEM((512, 384), F32),
-            pltpu.VMEM((2, 3, 6, 6, 16, 128), F32),
-        ]
-        + [pltpu.VMEM(*out) for out in outs]
-        + [pltpu.VMEM((6, 16, 128), F32)]
-        + [pltpu.SemaphoreType.DMA((n,)) for n in (6, 8, 5)],
-        in_specs=[smem] * 3 + [hbm] * 7,
-        out_specs=[hbm] * 5,
-        vmem=60,
-    )(tm.reshape(1), core.reshape(1), groups, prev, lat, near, far, cotangent, wide, tall)
+        scratch=[pltpu.VMEM(*x) for x in MAIN_SCRATCH] + [pltpu.SemaphoreType.DMA((8,))],
+        in_specs=[smem, smem] + [vmem] * 4 + [hbm] + [vmem] * 2,
+        out_specs=[vmem] * 5,
+        vmem=52,
+    )(core.reshape(1), masks, prev, lat, near, far, cotangent, wide, tall)
+    from_far = crossed(gfar)
     given = swapped(pair)
-    half = call(add_body, jax.ShapeDtypeStruct((64, 4, 384), BF), (1e5, 6e5), in_specs=[vmem] * 2)(keep, given)
-    from_far = crossed(gfar)
-    early = call(
-        early_body,
-        jax.ShapeDtypeStruct((2, 2, 4, 16, 128), BF),
-        (1e5, 3e5),
-        in_specs=[smem] + [vmem] * 3,
-    )(core.reshape(1), gprev, given, from_far)
+    half, early = call(
+        mix_body,
+        (jax.ShapeDtypeStruct((64, 4, 384), BF), jax.ShapeDtypeStruct((2, 2, 4, 16, 128), BF)),
+        (1e5, 1e6),
+        in_specs=[smem] + [vmem] * 4,
+    )(core.reshape(1), keep, given, gprev, from_far)
     from_next = shifted(early, -1)
     parts = exchange(half, CHIPS)
     part = jnp.sum(parts.astype(F32), axis=0)

time: 95.3 us -> 86.5 us (0.908)
  Pallas kernels: 23.5 us -> 17.6 us
  blocking collectives: 20.9 us -> 16.8 us
  waiting for transfers between devices: 10.9 us -> 13.8 us
    all_to_all x1, waiting for transfers between devices: 1.38 us -> 9.07 us  [exchange(): return lax.all_to_all(value, axes, split_axis=0, concat_axis=0, tiled=True)]
    all_to_all x1, blocking collectives: 20.9 us -> 16.8 us  [exchange(): return lax.all_to_all(value, axes, split_axis=0, concat_axis=0, tiled=True)]
    pallas_call x3, Pallas kernels: 17.6 us -> 13.5 us  [the longest x1 11.4 us: on_device(): call(main_body, tuple((jax.ShapeDtypeStruct(*out) for out in MAIN_OUTS)),...]
    ppermute x2, waiting for transfers between devices: 5.01 us -> 1.95 us  [crossed(): return lax.ppermute(value, BAND, pairs + [(j, i) for i, j in pairs])]
    pallas_call x1, Pallas kernels: 3.52 us -> 1.59 us  [on_device(): call(select_body, (jax.ShapeDtypeStruct((512, 128), jnp.int32), jax.Shape...]
    ppermute x3, waiting for transfers between devices: 2.97 us -> 1.26 us  [swapped(): return lax.ppermute(value, 'core', [(0, 1), (1, 0)])]
    unnamed x19 -> x7, local copies, waits for them, and re-layouts: 4.35 us -> 3.53 us
  transfers between devices with their start and end apart: 9 -> 9, of which waited for: 6 -> 4; matrix products, arithmetic and copies ran while one was open for 0% -> 0% of each run, Pallas kernels for 4% -> 3%
where the time goes in v2:
time: 86.5 us; the launch traced here: 86.1 us
  starting transfers between devices  33.5 us (39%)
  Pallas kernels  17.6 us (20%)
  blocking collectives  16.8 us (19%)
  waiting for transfers between devices  13.8 us (16%)
  local copies, waits for them, and re-layouts  3.57 us (4%)
    all_to_all x1, blocking collectives, exchange(): return lax.all_to_all(value, axes, split_axis=0, concat_axis=0, tiled=True)  16.8 us
    all_to_all x1, starting transfers between devices, exchange(): return lax.all_to_all(value, axes, split_axis=0, concat_axis=0, tiled=True)  12.8 us
    pallas_call x1, Pallas kernels, on_device(): call(main_body, tuple((jax.ShapeDtypeStruct(*out) for out in MAIN_OUTS)),...  11.4 us
    all_to_all x1, waiting for transfers between devices, exchange(): return lax.all_to_all(value, axes, split_axis=0, concat_axis=0, tiled=True)  9.07 us
    ppermute x2, starting transfers between devices, crossed(): return lax.ppermute(value, BAND, pairs + [(j, i) for i, j in pairs])  7.83 us
    ppermute x2, starting transfers between devices, shifted(): lax.ppermute(value, 'tm', [(i, i + step) for i in range(count) if 0 <= i...  5.33 us
    ppermute x3, starting transfers between devices, swapped(): return lax.ppermute(value, 'core', [(0, 1), (1, 0)])  5.01 us
    unnamed x7, local copies, waits for them, and re-layouts  3.53 us
  transfers between devices with their start and end apart: 9, of which 4 were waited for; matrix products, arithmetic and copies ran while one was open for 0% of the time, Pallas kernels for 3%

profile of v2, /device:TPU:1, one launch (start us, length us, event | category | flops | bytes accessed | tf_op | source)
XLA Modules:
  0.0 86.1 jit_solution(3978040826552304659)
XLA Ops:
  0.6 0.9 %copy.12 = bf16[2,16,4,4,128]{4,1,2,0,3:T(8,128)(2,1)S(1)} copy(bf16[2,16,4,4,128]{4,3,2,1,0:T(4,128)(2,1)} %param.5) | data formatting | bytes 262144 | tf_op args[0]
  1.6 4.0 %collective-permute-start = (bf16[4,2,2,16,128]{4,3,2,1,0:T(8,128)(2,1)S(1)}, bf16[4,2,2,16,128]{4,3,2,1,0:T(8,128)(2,1)S(1)}, u32[]{:S(2)}, u32[]{:S(2)}) collective-permute-start(bf16[4,2,2,16,128]{4,3,2,1,0:T(8,128)(2,1)S(1)} %slice.4), channel_id=1, source_target_pairs={{0,64},{64,128},{128,192},{1,65},{65,129},{129,193},{2,66},{66,130... | collective-permute-start | bytes 196616 | tf_op jit(solution)/shard_map/ppermute | solution.py:305
  5.6 0.0 copy-start
  5.7 1.0 %copy-done = bf16[384,432]{0,1:T(8,128)(2,1)S(1)} copy-done((bf16[384,432]{0,1:T(8,128)(2,1)S(1)}, bf16[384,432]{0,1:T(8,128)(2,1)}, u32[]{:S(2)}) %copy-start) | copy-done | bytes 331800
  6.6 0.0 copy-start.1
  6.6 0.7 copy-done.1
  7.3 1.3 %shard_map.68 = (bf16[384,512]{1,0:T(8,128)(2,1)S(1)}, bf16[432,384]{1,0:T(8,128)(2,1)S(1)}, s32[24]{0:T(128)S(1)}) custom-call(s32[1]{0:T(128)} %bitcast.2.me_ref, s32[2,16]{1,0:T(2,128)S(1)} %copy-done.1, bf16[432,384]{1,0:T(8,128)(2,1)S(1)} %bitcast.21), custom_call_target="tpu_custom_call" | custom-call | flops 1000000 | bytes 2000000 | tf_op jit(solution)/shard_map/pallas_call | solution.py:335
  8.6 0.0 collective-permute-done.prev
  8.7 4.4 %collective-permute-start.2 = (bf16[2,6,16,128]{3,2,1,0:T(8,128)(2,1)S(1)}, bf16[2,6,16,128]{3,2,1,0:T(8,128)(2,1)S(1)}, u32[]{:S(2)}, u32[]{:S(2)}) collective-permute-start(bf16[2,6,16,128]{3,2,1,0:T(8,128)(2,1)S(1)} %pad_maximum_fusion.1), channel_id=1, source_target_pairs={{2,4},{6,8},{10,12},{14,16},{18,20},{22,24},{26,28},{30,32},{34,36... | collective-permute-start | bytes 147464 | tf_op jit(solution)/shard_map/ppermute | solution.py:311
  13.1 0.1 collective-permute-start.1
  13.2 0.0 copy-start.2
  13.2 0.9 %copy-done.2 = s32[65536]{0:T(1024)S(1)} copy-done((s32[65536]{0:T(1024)S(1)}, s32[65536]{0:T(1024)}, u32[]{:S(2)}) %copy-start.2) | copy-done | bytes 262168
  14.2 1.6 %shard_map.69 = (s32[512,128]{1,0:T(8,128)S(1)}, s32[2,256,128]{2,1,0:T(8,128)S(1)}) custom-call(s32[1]{0:T(128)} %bitcast.2.me_ref, s32[512,128]{1,0:T(8,128)S(1)} %bitcast.22), custom_call_target="tpu_custom_call" | custom-call | flops 500000000 | bytes 2000000 | tf_op jit(solution)/shard_map/pallas_call | solution.py:352
  15.8 0.0 collective-permute-done.2.far
  15.8 0.0 collective-permute-done.1.near
  15.8 11.4 %shard_map.70 = (bf16[48,16,128]{2,1,0:T(8,128)(2,1)S(1)}, bf16[60,16,128]{2,1,0:T(8,128)(2,1)S(1)}, f32[2,4,4,16,128]{4,3,2,1,0:T(8,128)S(1)}, bf16[2,6,16,128]...) custom-call(s32[1]{0:T(128)} %bitcast.core_ref, s32[24]{0:T(128)S(1)} %get-tuple-element.21.mask_ref, ...), custom_call_target="tpu_custom_call" | custom-call | flops 4499999744 | bytes 5000000 | tf_op jit(solution)/shard_map/pallas_call | solution.py:361
  27.2 0.6 collective-permute-start.3
  27.8 3.4 %collective-permute-start.4 = (bf16[2,6,16,128]{3,2,1,0:T(8,128)(2,1)S(1)}, bf16[2,6,16,128]{3,2,1,0:T(8,128)(2,1)S(1)}, u32[]{:S(2)}, u32[]{:S(2)}) collective-permute-start(bf16[2,6,16,128]{3,2,1,0:T(8,128)(2,1)S(1)} %get-tuple-element.29), channel_id=1, source_target_pairs={{2,4},{6,8},{10,12},{14,16},{18,20},{22,24},{26,28},{30,32},{34,36... | collective-permute-start | bytes 147464 | tf_op jit(solution)/shard_map/ppermute | solution.py:311
  31.2 1.9 %collective-permute-done.4.far_ref = bf16[2,6,16,128]{3,2,1,0:T(8,128)(2,1)S(1)} collective-permute-done((bf16[2,6,16,128]{3,2,1,0:T(8,128)(2,1)S(1)}, bf16[2,6,16,128]{3,2,1,0:T(8,128)(2,1)S(1)}, u32[]{:S(2)}, u32[]{:S(2)}) %collective-permute-start.4) | collective-permute-done | bytes 49184 | tf_op jit(solution)/shard_map/ppermute | solution.py:311
  33.2 0.0 collective-permute-done.3.given_ref
  33.2 0.8 shard_map.71
  34.0 12.8 %all-to-all-start = ((bf16[64,4,384]{2,1,0:T(4,128)(2,1)}), bf16[64,4,384]{2,1,0:T(4,128)(2,1)S(1)}, u32[]{:S(2)}, u32[]{:S(2)}) async-start(bf16[64,4,384]{2,1,0:T(4,128)(2,1)} %get-tuple-element.34), calls=%async_computation | async-start | bytes 393216 | tf_op jit(solution)/shard_map/all_to_all | solution.py:319
  46.7 1.3 %collective-permute-start.5 = (bf16[2,2,4,16,128]{4,3,2,1,0:T(8,128)(2,1)S(1)}, bf16[2,2,4,16,128]{4,3,2,1,0:T(8,128)(2,1)S(1)}, u32[]{:S(2)}, u32[]{:S(2)}) collective-permute-start(bf16[2,2,4,16,128]{4,3,2,1,0:T(8,128)(2,1)S(1)} %get-tuple-element.32), channel_id=1, source_target_pairs={{64,0},{128,64},{192,128},{65,1},{129,65},{193,129},{66,2},{130,66... | collective-permute-start | bytes 196616 | tf_op jit(solution)/shard_map/ppermute | solution.py:305
  48.0 9.1 %all-to-all-done = bf16[64,4,384]{2,1,0:T(4,128)(2,1)S(1)} async-done(((bf16[64,4,384]{2,1,0:T(4,128)(2,1)}), bf16[64,4,384]{2,1,0:T(4,128)(2,1)S(1)}, u32[]{:S(2)}, u32[]{:S(2)}) %all-to-all-start) | async-done | bytes 196640 | tf_op jit(solution)/shard_map/all_to_all | solution.py:319
  57.1 0.1 convert_reduce_fusion.part_ref
  57.2 2.5 %collective-permute-start.6 = (f32[4,384]{1,0:T(4,128)S(1)}, f32[4,384]{1,0:T(4,128)S(1)}, u32[]{:S(2)}, u32[]{:S(2)}) collective-permute-start(f32[4,384]{1,0:T(4,128)S(1)} %convert_reduce_fusion.part_ref), channel_id=1, source_target_pairs={{0,1},{1,0},{2,3},{3,2},{4,5},{5,4},{6,7},{7,6},{8,9},{9,8},{10,11... | collective-permute-start | bytes 18440 | tf_op jit(solution)/shard_map/ppermute | solution.py:381
  59.8 0.0 collective-permute-done.5.next_ref
  59.8 1.5 %collective-permute-done.6.twin_ref = f32[4,384]{1,0:T(4,128)S(1)} collective-permute-done((f32[4,384]{1,0:T(4,128)S(1)}, f32[4,384]{1,0:T(4,128)S(1)}, u32[]{:S(2)}, u32[]{:S(2)}) %collective-permute-start.6) | collective-permute-done | bytes 6176 | tf_op jit(solution)/shard_map/ppermute | solution.py:381
  61.3 0.6 shard_map.72
  61.9 16.8 %all_to_all.10.mine_ref = bf16[64,5,4,128]{3,2,1,0:T(4,128)(2,1)S(1)} all-to-all(bf16[64,5,4,128]{3,2,1,0:T(4,128)(2,1)S(1)} %shard_map.72), channel_id=1, replica_groups=mesh['tm'=4,'xl'=2,'z'=8,'core'=2,'rep'=2] {'tm','xl','z'}, dimensions={0} | all-to-all | bytes 655360 | tf_op jit(solution)/shard_map/all_to_all | solution.py:319
  78.7 4.3 %collective-permute-start.7 = (bf16[64,5,4,128]{3,2,1,0:T(4,128)(2,1)S(1)}, bf16[64,5,4,128]{3,2,1,0:T(4,128)(2,1)S(1)}, u32[]{:S(2)}, u32[]{:S(2)}) collective-permute-start(bf16[64,5,4,128]{3,2,1,0:T(4,128)(2,1)S(1)} %all_to_all.10.mine_ref), channel_id=1, source_target_pairs={{0,2},{2,0},{1,3},{3,1},{4,6},{6,4},{5,7},{7,5},{8,10},{10,8},{9,1... | collective-permute-start | bytes 983048 | tf_op jit(solution)/shard_map/ppermute | solution.py:315
  83.0 1.3 %collective-permute-done.7.other_ref = bf16[64,5,4,128]{3,2,1,0:T(4,128)(2,1)S(1)} collective-permute-done((bf16[64,5,4,128]{3,2,1,0:T(4,128)(2,1)S(1)}, bf16[64,5,4,128]{3,2,1,0:T(4,128)(2,1)S(1)}, u32[]{:S(2)}, u32[]{:S(2)}) %collective-permute-start.7) | collective-permute-done | bytes 327712 | tf_op jit(solution)/shard_map/ppermute | solution.py:315
  84.3 1.9 %shard_map.73 = (bf16[2,256,128]{2,1,0:T(8,128)(2,1)}, f32[432,384]{1,0:T(8,128)}) custom-call(s32[1]{0:T(128)} %bitcast.core_ref, bf16[64,5,4,128]{3,2,1,0:T(4,128)(2,1)S(1)} %all_to_all.10.mine_ref, bf16[64,5,4,128]{3,2,1,0:T(4,128)(2,1)S(1)} %collective-permute-done.7.other_ref, s32[2,256,128]{2,1,0:T(8,128)S(1)} %get-tuple-element.35.take_ref), custom_call_target="tpu_custom_call" | custom-call | flops 200000000 | bytes 1000000 | tf_op jit(solution)/shard_map/pallas_call | solution.py:391
  (5 shorter events, 0.0 us)
Async XLA Ops:
  1.6 7.1 %collective-permute-start = (bf16[4,2,2,16,128]{4,3,2,1,0:T(8,128)(2,1)S(1)}, bf16[4,2,2,16,128]{4,3,2,1,0:T(8,128)(2,1)S(1)}, u32[]{:S(2)}, u32[]{:S(2)}) collective-permute-start(bf16[4,2,2,16,128]{4,3,2,1,0:T(8,128)(2,1)S(1)} %slice.4), channel_id=1, source_target_pairs={{0,64},{64,128},{128,192},{1,65},{65,129},{129,193},{2,66},{66,130... | collective-permute-start | bytes 196616 | tf_op jit(solution)/shard_map/ppermute | solution.py:305
  5.6 1.0 %copy-start = (bf16[384,432]{0,1:T(8,128)(2,1)S(1)}, bf16[384,432]{0,1:T(8,128)(2,1)}, u32[]{:S(2)}) copy-start(bf16[384,432]{0,1:T(8,128)(2,1)} %param.6) | copy-start | bytes 995332
  6.6 0.7 copy-start.1
  8.7 7.1 %collective-permute-start.2 = (bf16[2,6,16,128]{3,2,1,0:T(8,128)(2,1)S(1)}, bf16[2,6,16,128]{3,2,1,0:T(8,128)(2,1)S(1)}, u32[]{:S(2)}, u32[]{:S(2)}) collective-permute-start(bf16[2,6,16,128]{3,2,1,0:T(8,128)(2,1)S(1)} %pad_maximum_fusion.1), channel_id=1, source_target_pairs={{2,4},{6,8},{10,12},{14,16},{18,20},{22,24},{26,28},{30,32},{34,36... | collective-permute-start | bytes 147464 | tf_op jit(solution)/shard_map/ppermute | solution.py:311
  13.1 2.7 %collective-permute-start.1 = (bf16[2,6,16,128]{3,2,1,0:T(8,128)(2,1)S(1)}, bf16[2,6,16,128]{3,2,1,0:T(8,128)(2,1)S(1)}, u32[]{:S(2)}, u32[]{:S(2)}) collective-permute-start(bf16[2,6,16,128]{3,2,1,0:T(8,128)(2,1)S(1)} %pad_maximum_fusion), channel_id=1, source_target_pairs={{0,2},{2,0},{1,3},{3,1},{4,6},{6,4},{5,7},{7,5},{8,10},{10,8},{9,1... | collective-permute-start | bytes 147464 | tf_op jit(solution)/shard_map/ppermute | solution.py:315
  13.2 1.0 %copy-start.2 = (s32[65536]{0:T(1024)S(1)}, s32[65536]{0:T(1024)}, u32[]{:S(2)}) copy-start(s32[65536]{0:T(1024)} %param.9) | copy-start | bytes 786436
  27.2 6.0 %collective-permute-start.3 = (bf16[60,16,128]{2,1,0:T(8,128)(2,1)S(1)}, bf16[60,16,128]{2,1,0:T(8,128)(2,1)S(1)}, u32[]{:S(2)}, u32[]{:S(2)}) collective-permute-start(bf16[60,16,128]{2,1,0:T(8,128)(2,1)S(1)} %get-tuple-element.28), channel_id=1, source_target_pairs={{0,2},{2,0},{1,3},{3,1},{4,6},{6,4},{5,7},{7,5},{8,10},{10,8},{9,1... | collective-permute-start | bytes 737288 | tf_op jit(solution)/shard_map/ppermute | solution.py:315
  27.8 5.4 %collective-permute-start.4 = (bf16[2,6,16,128]{3,2,1,0:T(8,128)(2,1)S(1)}, bf16[2,6,16,128]{3,2,1,0:T(8,128)(2,1)S(1)}, u32[]{:S(2)}, u32[]{:S(2)}) collective-permute-start(bf16[2,6,16,128]{3,2,1,0:T(8,128)(2,1)S(1)} %get-tuple-element.29), channel_id=1, source_target_pairs={{2,4},{6,8},{10,12},{14,16},{18,20},{22,24},{26,28},{30,32},{34,36... | collective-permute-start | bytes 147464 | tf_op jit(solution)/shard_map/ppermute | solution.py:311
  34.0 23.1 %all-to-all-start = ((bf16[64,4,384]{2,1,0:T(4,128)(2,1)}), bf16[64,4,384]{2,1,0:T(4,128)(2,1)S(1)}, u32[]{:S(2)}, u32[]{:S(2)}) async-start(bf16[64,4,384]{2,1,0:T(4,128)(2,1)} %get-tuple-element.34), calls=%async_computation | async-start | bytes 393216 | tf_op jit(solution)/shard_map/all_to_all | solution.py:319
  46.7 13.0 %collective-permute-start.5 = (bf16[2,2,4,16,128]{4,3,2,1,0:T(8,128)(2,1)S(1)}, bf16[2,2,4,16,128]{4,3,2,1,0:T(8,128)(2,1)S(1)}, u32[]{:S(2)}, u32[]{:S(2)}) collective-permute-start(bf16[2,2,4,16,128]{4,3,2,1,0:T(8,128)(2,1)S(1)} %get-tuple-element.32), channel_id=1, source_target_pairs={{64,0},{128,64},{192,128},{65,1},{129,65},{193,129},{66,2},{130,66... | collective-permute-start | bytes 196616 | tf_op jit(solution)/shard_map/ppermute | solution.py:305
  57.2 4.1 %collective-permute-start.6 = (f32[4,384]{1,0:T(4,128)S(1)}, f32[4,384]{1,0:T(4,128)S(1)}, u32[]{:S(2)}, u32[]{:S(2)}) collective-permute-start(f32[4,384]{1,0:T(4,128)S(1)} %convert_reduce_fusion.part_ref), channel_id=1, source_target_pairs={{0,1},{1,0},{2,3},{3,2},{4,5},{5,4},{6,7},{7,6},{8,9},{9,8},{10,11... | collective-permute-start | bytes 18440 | tf_op jit(solution)/shard_map/ppermute | solution.py:381
  78.7 5.6 %collective-permute-start.7 = (bf16[64,5,4,128]{3,2,1,0:T(4,128)(2,1)S(1)}, bf16[64,5,4,128]{3,2,1,0:T(4,128)(2,1)S(1)}, u32[]{:S(2)}, u32[]{:S(2)}) collective-permute-start(bf16[64,5,4,128]{3,2,1,0:T(4,128)(2,1)S(1)} %all_to_all.10.mine_ref), channel_id=1, source_target_pairs={{0,2},{2,0},{1,3},{3,1},{4,6},{6,4},{5,7},{7,5},{8,10},{10,8},{9,1... | collective-permute-start | bytes 983048 | tf_op jit(solution)/shard_map/ppermute | solution.py:315

commit v3 on v2

--- a/solution.py
+++ b/solution.py
@@ -41,6 +41,8 @@
     ((1536, 128), F32),
     ((384, 512), BF),
     ((512, 384), F32),
+    ((512, 512), BF),
+    ((384, 512), F32),
 ]
 
 
@@ -124,7 +126,7 @@
 
 def main_body(
     core_ref, mask_ref, prev, lat, near, far, cot_hbm, wide, wt, keep, pair, own, gfar, gprev,
-    cot, ext, patch, pre, total, spread, edges, cots, grad, turned, cot_sems,
+    cot, ext, patch, pre, total, spread, edges, cots, grad, turned, patch1, pre1, cot_sems,
 ):
     lanes = lax.broadcasted_iota(jnp.int32, (1, 128), 1)
     near_row = 5 - 5 * core_ref[0]
@@ -135,6 +137,7 @@
     for i in range(8):
         cot_copy(i).start()
     patch[432:512, :] = jnp.zeros((80, 512), BF)
+    patch1[432:512, :] = jnp.zeros((80, 512), BF)
     total[...] = jnp.zeros_like(total)
     spread[...] = jnp.zeros_like(spread)
     for b in range(2):
@@ -153,7 +156,7 @@
     def factors(i):
         return [mask_ref[3 * i + a].astype(F32) for a in range(3)]
 
-    def build(i):
+    def build(i, patch):
         b, f = i >> 2, i & 3
         masks = factors(i)
         for a in range(3):
@@ -168,7 +171,7 @@
         cot_copy(i).wait()
         cots[...] = cot[i].astype(F32).reshape(1536, 128)
 
-    def elements(h):
+    def elements(h, pre):
         x = pre[:, h * 128 : h * 128 + 128]
         t = jnp.tanh(x)
         cot = cots[pl.ds(h, 384, stride=4), :]
@@ -188,19 +191,26 @@
                         acc = term if acc is None else acc + term
                 spread[b, c, f + a, row] += acc * mask
 
-    def step(i, carry):
-        build(i)
+    def advance(i, patch, pre, next_patch, next_pre):
+        build(jnp.minimum(i + 1, 7), next_patch)
         relayout(i)
-        pre[...] = matmul(wide[...], patch[...])
+        next_pre[...] = matmul(wide[...], next_patch[...])
         for h in range(4):
-            elements(h)
+            elements(h, pre)
         back = matmul(wt[...], grad[...])
         total[...] += matmul_nt(grad[...], patch[...])
         for a in range(3):
             spread_tap(i, a, back[a * 144 : a * 144 + 144])
+
+    build(0, patch)
+    pre[...] = matmul(wide[...], patch[...])
+
+    def step(j, carry):
+        advance(2 * j, patch, pre, patch1, pre1)
+        advance(2 * j + 1, patch1, pre1, patch, pre)
         return carry
 
-    lax.fori_loop(0, 8, step, 0)
+    lax.fori_loop(0, 4, step, 0)
     turned[...] = total[...].T
     mine = core_ref[0] * 256
     for g in range(16):
@@ -228,19 +238,22 @@
                 own[b, fr - 2] = x[1:5]
 
 
-def mix_body(core_ref, keep_ref, given_ref, gprev_ref, far_ref, half_ref, early_ref):
+def add_body(keep_ref, given_ref, out_ref):
     for g in range(16):
         for i in range(3):
             x = keep_ref[g * 3 + i].astype(F32) + given_ref[g * 3 + i].astype(F32)
-            half_ref[g * 4 : g * 4 + 4, :, i * 128 : i * 128 + 128] = x.reshape(4, 4, 128).astype(BF)
+            out_ref[g * 4 : g * 4 + 4, :, i * 128 : i * 128 + 128] = x.reshape(4, 4, 128).astype(BF)
+
+
+def early_body(core_ref, gprev_ref, given_ref, far_ref, out_ref):
     near_row = 3 - 3 * core_ref[0]
-    early_ref[...] = gprev_ref[...].astype(BF)
+    out_ref[...] = gprev_ref[...].astype(BF)
     for b in range(2):
         for f in range(2):
             near = given_ref[48 + b * 6 + f].astype(F32)
-            early_ref[b, f, near_row] = (gprev_ref[b, f, near_row] + near).astype(BF)
+            out_ref[b, f, near_row] = (gprev_ref[b, f, near_row] + near).astype(BF)
             far = far_ref[b, f].astype(F32)
-            early_ref[b, f, 3 - near_row] = (gprev_ref[b, f, 3 - near_row] + far).astype(BF)
+            out_ref[b, f, 3 - near_row] = (gprev_ref[b, f, 3 - near_row] + far).astype(BF)
 
 
 def out_body(core_ref, own_ref, given_ref, far_ref, next_ref, send_ref, part_ref, twin_ref, out_ref, rows, grad):
@@ -369,12 +382,13 @@
     )(core.reshape(1), masks, prev, lat, near, far, cotangent, wide, tall)
     from_far = crossed(gfar)
     given = swapped(pair)
-    half, early = call(
-        mix_body,
-        (jax.ShapeDtypeStruct((64, 4, 384), BF), jax.ShapeDtypeStruct((2, 2, 4, 16, 128), BF)),
-        (1e5, 1e6),
-        in_specs=[smem] + [vmem] * 4,
-    )(core.reshape(1), keep, given, gprev, from_far)
+    half = call(add_body, jax.ShapeDtypeStruct((64, 4, 384), BF), (1e5, 3e7), in_specs=[vmem] * 2)(keep, given)
+    early = call(
+        early_body,
+        jax.ShapeDtypeStruct((2, 2, 4, 16, 128), BF),
+        (1e5, 3e5),
+        in_specs=[smem] + [vmem] * 3,
+    )(core.reshape(1), gprev, given, from_far)
     from_next = shifted(early, -1)
     parts = exchange(half, CHIPS)
     part = jnp.sum(parts.astype(F32), axis=0)

time: 86.5 us -> 83.5 us (0.965)
  waiting for transfers between devices: 13.8 us -> 9.31 us
  blocking collectives: 16.8 us -> 20 us
  Pallas kernels: 17.6 us -> 15.8 us
    all_to_all x1, waiting for transfers between devices: 9.07 us -> 2.29 us  [exchange(): return lax.all_to_all(value, axes, split_axis=0, concat_axis=0, tiled=True)]
    all_to_all x1, blocking collectives: 16.8 us -> 20 us  [exchange(): return lax.all_to_all(value, axes, split_axis=0, concat_axis=0, tiled=True)]
    pallas_call x1, Pallas kernels: 11.4 us -> 9.68 us  [on_device(): call(main_body, tuple((jax.ShapeDtypeStruct(*out) for out in MAIN_OUTS)),...]
    ppermute x2, waiting for transfers between devices: 1.95 us -> 3.09 us  [crossed(): return lax.ppermute(value, BAND, pairs + [(j, i) for i, j in pairs])]
    ppermute x3, waiting for transfers between devices: 1.26 us -> 2.4 us  [swapped(): return lax.ppermute(value, 'core', [(0, 1), (1, 0)])]
  transfers between devices with their start and end apart: 9 -> 9, of which waited for: 4 -> 5; matrix products, arithmetic and copies ran while one was open for 0% -> 0% of each run, Pallas kernels for 3% -> 4%
where the time goes in v3:
time: 83.5 us; the launch traced here: 83.1 us
  starting transfers between devices  33.5 us (40%)
  blocking collectives  20 us (24%)
  Pallas kernels  15.8 us (19%)
  waiting for transfers between devices  9.31 us (11%)
  local copies, waits for them, and re-layouts  3.57 us (4%)
    all_to_all x1, blocking collectives, exchange(): return lax.all_to_all(value, axes, split_axis=0, concat_axis=0, tiled=True)  20 us
    all_to_all x1, starting transfers between devices, exchange(): return lax.all_to_all(value, axes, split_axis=0, concat_axis=0, tiled=True)  12.5 us
    pallas_call x1, Pallas kernels, on_device(): call(main_body, tuple((jax.ShapeDtypeStruct(*out) for out in MAIN_OUTS)),...  9.68 us
    ppermute x2, starting transfers between devices, crossed(): return lax.ppermute(value, BAND, pairs + [(j, i) for i, j in pairs])  8.13 us
    ppermute x2, starting transfers between devices, shifted(): lax.ppermute(value, 'tm', [(i, i + step) for i in range(count) if 0 <= i...  5.33 us
    ppermute x3, starting transfers between devices, swapped(): return lax.ppermute(value, 'core', [(0, 1), (1, 0)])  5.05 us
    unnamed x7, local copies, waits for them, and re-layouts  3.53 us
    ppermute x2, waiting for transfers between devices, crossed(): return lax.ppermute(value, BAND, pairs + [(j, i) for i, j in pairs])  3.09 us
  transfers between devices with their start and end apart: 9, of which 5 were waited for; matrix products, arithmetic and copies ran while one was open for 0% of the time, Pallas kernels for 4%

profile of v3, /device:TPU:1, one launch (start us, length us, event | category | flops | bytes accessed | tf_op | source)
XLA Modules:
  0.0 83.1 jit_solution(8171810189561128122)
XLA Ops:
  0.6 0.9 %copy.12 = bf16[2,16,4,4,128]{4,1,2,0,3:T(8,128)(2,1)S(1)} copy(bf16[2,16,4,4,128]{4,3,2,1,0:T(4,128)(2,1)} %param.5) | data formatting | bytes 262144 | tf_op args[0]
  1.6 4.0 %collective-permute-start = (bf16[4,2,2,16,128]{4,3,2,1,0:T(8,128)(2,1)S(1)}, bf16[4,2,2,16,128]{4,3,2,1,0:T(8,128)(2,1)S(1)}, u32[]{:S(2)}, u32[]{:S(2)}) collective-permute-start(bf16[4,2,2,16,128]{4,3,2,1,0:T(8,128)(2,1)S(1)} %slice.4), channel_id=1, source_target_pairs={{0,64},{64,128},{128,192},{1,65},{65,129},{129,193},{2,66},{66,130... | collective-permute-start | bytes 196616 | tf_op jit(solution)/shard_map/ppermute | solution.py:318
  5.6 0.0 copy-start
  5.7 1.0 %copy-done = bf16[384,432]{0,1:T(8,128)(2,1)S(1)} copy-done((bf16[384,432]{0,1:T(8,128)(2,1)S(1)}, bf16[384,432]{0,1:T(8,128)(2,1)}, u32[]{:S(2)}) %copy-start) | copy-done | bytes 331800
  6.6 0.0 copy-start.1
  6.6 0.7 copy-done.1
  7.3 1.3 %shard_map.68 = (bf16[384,512]{1,0:T(8,128)(2,1)S(1)}, bf16[432,384]{1,0:T(8,128)(2,1)S(1)}, s32[24]{0:T(128)S(1)}) custom-call(s32[1]{0:T(128)} %bitcast.2.me_ref, s32[2,16]{1,0:T(2,128)S(1)} %copy-done.1, bf16[432,384]{1,0:T(8,128)(2,1)S(1)} %bitcast.21), custom_call_target="tpu_custom_call" | custom-call | flops 1000000 | bytes 2000000 | tf_op jit(solution)/shard_map/pallas_call | solution.py:348
  8.6 0.0 collective-permute-done.prev
  8.7 4.4 %collective-permute-start.2 = (bf16[2,6,16,128]{3,2,1,0:T(8,128)(2,1)S(1)}, bf16[2,6,16,128]{3,2,1,0:T(8,128)(2,1)S(1)}, u32[]{:S(2)}, u32[]{:S(2)}) collective-permute-start(bf16[2,6,16,128]{3,2,1,0:T(8,128)(2,1)S(1)} %pad_maximum_fusion.1), channel_id=1, source_target_pairs={{2,4},{6,8},{10,12},{14,16},{18,20},{22,24},{26,28},{30,32},{34,36... | collective-permute-start | bytes 147464 | tf_op jit(solution)/shard_map/ppermute | solution.py:324
  13.1 0.1 collective-permute-start.1
  13.2 0.0 copy-start.2
  13.2 0.9 %copy-done.2 = s32[65536]{0:T(1024)S(1)} copy-done((s32[65536]{0:T(1024)S(1)}, s32[65536]{0:T(1024)}, u32[]{:S(2)}) %copy-start.2) | copy-done | bytes 262168
  14.2 1.6 %shard_map.69 = (s32[512,128]{1,0:T(8,128)S(1)}, s32[2,256,128]{2,1,0:T(8,128)S(1)}) custom-call(s32[1]{0:T(128)} %bitcast.2.me_ref, s32[512,128]{1,0:T(8,128)S(1)} %bitcast.22), custom_call_target="tpu_custom_call" | custom-call | flops 500000000 | bytes 2000000 | tf_op jit(solution)/shard_map/pallas_call | solution.py:365
  15.8 0.0 collective-permute-done.2.far
  15.8 0.0 collective-permute-done.1.near
  15.8 9.7 %shard_map.70 = (bf16[48,16,128]{2,1,0:T(8,128)(2,1)S(1)}, bf16[60,16,128]{2,1,0:T(8,128)(2,1)S(1)}, f32[2,4,4,16,128]{4,3,2,1,0:T(8,128)S(1)}, bf16[2,6,16,128]...) custom-call(s32[1]{0:T(128)} %bitcast.core_ref, s32[24]{0:T(128)S(1)} %get-tuple-element.19.mask_ref, ...), custom_call_target="tpu_custom_call" | custom-call | flops 4499999744 | bytes 5000000 | tf_op jit(solution)/shard_map/pallas_call | solution.py:374
  25.5 0.6 collective-permute-start.3
  26.1 1.1 %collective-permute-done.3.given_ref = bf16[60,16,128]{2,1,0:T(8,128)(2,1)S(1)} collective-permute-done((bf16[60,16,128]{2,1,0:T(8,128)(2,1)S(1)}, bf16[60,16,128]{2,1,0:T(8,128)(2,1)S(1)}, u32[]{:S(2)}, u32[]{:S(2)}) %collective-permute-start.3) | collective-permute-done | bytes 245792 | tf_op jit(solution)/shard_map/ppermute | solution.py:328
  27.2 0.8 shard_map.72
  28.0 12.5 %all-to-all-start = ((bf16[64,4,384]{2,1,0:T(4,128)(2,1)}), bf16[64,4,384]{2,1,0:T(4,128)(2,1)S(1)}, u32[]{:S(2)}, u32[]{:S(2)}) async-start(bf16[64,4,384]{2,1,0:T(4,128)(2,1)} %shard_map.72), calls=%async_computation | async-start | bytes 393216 | tf_op jit(solution)/shard_map/all_to_all | solution.py:332
  40.4 3.7 %collective-permute-start.4 = (bf16[2,6,16,128]{3,2,1,0:T(8,128)(2,1)S(1)}, bf16[2,6,16,128]{3,2,1,0:T(8,128)(2,1)S(1)}, u32[]{:S(2)}, u32[]{:S(2)}) collective-permute-start(bf16[2,6,16,128]{3,2,1,0:T(8,128)(2,1)S(1)} %get-tuple-element.27), channel_id=1, source_target_pairs={{2,4},{6,8},{10,12},{14,16},{18,20},{22,24},{26,28},{30,32},{34,36... | collective-permute-start | bytes 147464 | tf_op jit(solution)/shard_map/ppermute | solution.py:324
  44.2 3.1 %collective-permute-done.4.far_ref = bf16[2,6,16,128]{3,2,1,0:T(8,128)(2,1)S(1)} collective-permute-done((bf16[2,6,16,128]{3,2,1,0:T(8,128)(2,1)S(1)}, bf16[2,6,16,128]{3,2,1,0:T(8,128)(2,1)S(1)}, u32[]{:S(2)}, u32[]{:S(2)}) %collective-permute-start.4) | collective-permute-done | bytes 49184 | tf_op jit(solution)/shard_map/ppermute | solution.py:324
  47.3 1.3 %collective-permute-start.5 = (bf16[2,2,4,16,128]{4,3,2,1,0:T(8,128)(2,1)S(1)}, bf16[2,2,4,16,128]{4,3,2,1,0:T(8,128)(2,1)S(1)}, u32[]{:S(2)}, u32[]{:S(2)}) collective-permute-start(bf16[2,2,4,16,128]{4,3,2,1,0:T(8,128)(2,1)S(1)} %shard_map.71), channel_id=1, source_target_pairs={{64,0},{128,64},{192,128},{65,1},{129,65},{193,129},{66,2},{130,66... | collective-permute-start | bytes 196616 | tf_op jit(solution)/shard_map/ppermute | solution.py:318
  48.6 2.3 %all-to-all-done = bf16[64,4,384]{2,1,0:T(4,128)(2,1)S(1)} async-done(((bf16[64,4,384]{2,1,0:T(4,128)(2,1)}), bf16[64,4,384]{2,1,0:T(4,128)(2,1)S(1)}, u32[]{:S(2)}, u32[]{:S(2)}) %all-to-all-start) | async-done | bytes 196640 | tf_op jit(solution)/shard_map/all_to_all | solution.py:332
  50.9 0.1 convert_reduce_fusion.part_ref
  51.0 2.5 %collective-permute-start.6 = (f32[4,384]{1,0:T(4,128)S(1)}, f32[4,384]{1,0:T(4,128)S(1)}, u32[]{:S(2)}, u32[]{:S(2)}) collective-permute-start(f32[4,384]{1,0:T(4,128)S(1)} %convert_reduce_fusion.part_ref), channel_id=1, source_target_pairs={{0,1},{1,0},{2,3},{3,2},{4,5},{5,4},{6,7},{7,6},{8,9},{9,8},{10,11... | collective-permute-start | bytes 18440 | tf_op jit(solution)/shard_map/ppermute | solution.py:395
  53.5 0.0 collective-permute-done.5.next_ref
  53.5 1.5 %collective-permute-done.6.twin_ref = f32[4,384]{1,0:T(4,128)S(1)} collective-permute-done((f32[4,384]{1,0:T(4,128)S(1)}, f32[4,384]{1,0:T(4,128)S(1)}, u32[]{:S(2)}, u32[]{:S(2)}) %collective-permute-start.6) | collective-permute-done | bytes 6176 | tf_op jit(solution)/shard_map/ppermute | solution.py:395
  55.0 0.6 shard_map.73
  55.7 20.0 %all_to_all.10.mine_ref = bf16[64,5,4,128]{3,2,1,0:T(4,128)(2,1)S(1)} all-to-all(bf16[64,5,4,128]{3,2,1,0:T(4,128)(2,1)S(1)} %shard_map.73), channel_id=1, replica_groups=mesh['tm'=4,'xl'=2,'z'=8,'core'=2,'rep'=2] {'tm','xl','z'}, dimensions={0} | all-to-all | bytes 655360 | tf_op jit(solution)/shard_map/all_to_all | solution.py:332
  75.6 4.4 %collective-permute-start.7 = (bf16[64,5,4,128]{3,2,1,0:T(4,128)(2,1)S(1)}, bf16[64,5,4,128]{3,2,1,0:T(4,128)(2,1)S(1)}, u32[]{:S(2)}, u32[]{:S(2)}) collective-permute-start(bf16[64,5,4,128]{3,2,1,0:T(4,128)(2,1)S(1)} %all_to_all.10.mine_ref), channel_id=1, source_target_pairs={{0,2},{2,0},{1,3},{3,1},{4,6},{6,4},{5,7},{7,5},{8,10},{10,8},{9,1... | collective-permute-start | bytes 983048 | tf_op jit(solution)/shard_map/ppermute | solution.py:328
  80.0 1.3 %collective-permute-done.7.other_ref = bf16[64,5,4,128]{3,2,1,0:T(4,128)(2,1)S(1)} collective-permute-done((bf16[64,5,4,128]{3,2,1,0:T(4,128)(2,1)S(1)}, bf16[64,5,4,128]{3,2,1,0:T(4,128)(2,1)S(1)}, u32[]{:S(2)}, u32[]{:S(2)}) %collective-permute-start.7) | collective-permute-done | bytes 327712 | tf_op jit(solution)/shard_map/ppermute | solution.py:328
  81.3 1.8 %shard_map.74 = (bf16[2,256,128]{2,1,0:T(8,128)(2,1)}, f32[432,384]{1,0:T(8,128)}) custom-call(s32[1]{0:T(128)} %bitcast.core_ref, bf16[64,5,4,128]{3,2,1,0:T(4,128)(2,1)S(1)} %all_to_all.10.mine_ref, bf16[64,5,4,128]{3,2,1,0:T(4,128)(2,1)S(1)} %collective-permute-done.7.other_ref, s32[2,256,128]{2,1,0:T(8,128)S(1)} %get-tuple-element.31.take_ref), custom_call_target="tpu_custom_call" | custom-call | flops 200000000 | bytes 1000000 | tf_op jit(solution)/shard_map/pallas_call | solution.py:405
  (6 shorter events, 0.1 us)
Async XLA Ops:
  1.6 7.1 %collective-permute-start = (bf16[4,2,2,16,128]{4,3,2,1,0:T(8,128)(2,1)S(1)}, bf16[4,2,2,16,128]{4,3,2,1,0:T(8,128)(2,1)S(1)}, u32[]{:S(2)}, u32[]{:S(2)}) collective-permute-start(bf16[4,2,2,16,128]{4,3,2,1,0:T(8,128)(2,1)S(1)} %slice.4), channel_id=1, source_target_pairs={{0,64},{64,128},{128,192},{1,65},{65,129},{129,193},{2,66},{66,130... | collective-permute-start | bytes 196616 | tf_op jit(solution)/shard_map/ppermute | solution.py:318
  5.6 1.0 %copy-start = (bf16[384,432]{0,1:T(8,128)(2,1)S(1)}, bf16[384,432]{0,1:T(8,128)(2,1)}, u32[]{:S(2)}) copy-start(bf16[384,432]{0,1:T(8,128)(2,1)} %param.6) | copy-start | bytes 995332
  6.6 0.7 copy-start.1
  8.7 7.1 %collective-permute-start.2 = (bf16[2,6,16,128]{3,2,1,0:T(8,128)(2,1)S(1)}, bf16[2,6,16,128]{3,2,1,0:T(8,128)(2,1)S(1)}, u32[]{:S(2)}, u32[]{:S(2)}) collective-permute-start(bf16[2,6,16,128]{3,2,1,0:T(8,128)(2,1)S(1)} %pad_maximum_fusion.1), channel_id=1, source_target_pairs={{2,4},{6,8},{10,12},{14,16},{18,20},{22,24},{26,28},{30,32},{34,36... | collective-permute-start | bytes 147464 | tf_op jit(solution)/shard_map/ppermute | solution.py:324
  13.1 2.7 %collective-permute-start.1 = (bf16[2,6,16,128]{3,2,1,0:T(8,128)(2,1)S(1)}, bf16[2,6,16,128]{3,2,1,0:T(8,128)(2,1)S(1)}, u32[]{:S(2)}, u32[]{:S(2)}) collective-permute-start(bf16[2,6,16,128]{3,2,1,0:T(8,128)(2,1)S(1)} %pad_maximum_fusion), channel_id=1, source_target_pairs={{0,2},{2,0},{1,3},{3,1},{4,6},{6,4},{5,7},{7,5},{8,10},{10,8},{9,1... | collective-permute-start | bytes 147464 | tf_op jit(solution)/shard_map/ppermute | solution.py:328
  13.2 1.0 %copy-start.2 = (s32[65536]{0:T(1024)S(1)}, s32[65536]{0:T(1024)}, u32[]{:S(2)}) copy-start(s32[65536]{0:T(1024)} %param.9) | copy-start | bytes 786436
  25.5 1.7 %collective-permute-start.3 = (bf16[60,16,128]{2,1,0:T(8,128)(2,1)S(1)}, bf16[60,16,128]{2,1,0:T(8,128)(2,1)S(1)}, u32[]{:S(2)}, u32[]{:S(2)}) collective-permute-start(bf16[60,16,128]{2,1,0:T(8,128)(2,1)S(1)} %get-tuple-element.26), channel_id=1, source_target_pairs={{0,2},{2,0},{1,3},{3,1},{4,6},{6,4},{5,7},{7,5},{8,10},{10,8},{9,1... | collective-permute-start | bytes 737288 | tf_op jit(solution)/shard_map/ppermute | solution.py:328
  28.0 22.9 %all-to-all-start = ((bf16[64,4,384]{2,1,0:T(4,128)(2,1)}), bf16[64,4,384]{2,1,0:T(4,128)(2,1)S(1)}, u32[]{:S(2)}, u32[]{:S(2)}) async-start(bf16[64,4,384]{2,1,0:T(4,128)(2,1)} %shard_map.72), calls=%async_computation | async-start | bytes 393216 | tf_op jit(solution)/shard_map/all_to_all | solution.py:332
  40.4 6.8 %collective-permute-start.4 = (bf16[2,6,16,128]{3,2,1,0:T(8,128)(2,1)S(1)}, bf16[2,6,16,128]{3,2,1,0:T(8,128)(2,1)S(1)}, u32[]{:S(2)}, u32[]{:S(2)}) collective-permute-start(bf16[2,6,16,128]{3,2,1,0:T(8,128)(2,1)S(1)} %get-tuple-element.27), channel_id=1, source_target_pairs={{2,4},{6,8},{10,12},{14,16},{18,20},{22,24},{26,28},{30,32},{34,36... | collective-permute-start | bytes 147464 | tf_op jit(solution)/shard_map/ppermute | solution.py:324
  47.3 6.2 %collective-permute-start.5 = (bf16[2,2,4,16,128]{4,3,2,1,0:T(8,128)(2,1)S(1)}, bf16[2,2,4,16,128]{4,3,2,1,0:T(8,128)(2,1)S(1)}, u32[]{:S(2)}, u32[]{:S(2)}) collective-permute-start(bf16[2,2,4,16,128]{4,3,2,1,0:T(8,128)(2,1)S(1)} %shard_map.71), channel_id=1, source_target_pairs={{64,0},{128,64},{192,128},{65,1},{129,65},{193,129},{66,2},{130,66... | collective-permute-start | bytes 196616 | tf_op jit(solution)/shard_map/ppermute | solution.py:318
  51.0 4.1 %collective-permute-start.6 = (f32[4,384]{1,0:T(4,128)S(1)}, f32[4,384]{1,0:T(4,128)S(1)}, u32[]{:S(2)}, u32[]{:S(2)}) collective-permute-start(f32[4,384]{1,0:T(4,128)S(1)} %convert_reduce_fusion.part_ref), channel_id=1, source_target_pairs={{0,1},{1,0},{2,3},{3,2},{4,5},{5,4},{6,7},{7,6},{8,9},{9,8},{10,11... | collective-permute-start | bytes 18440 | tf_op jit(solution)/shard_map/ppermute | solution.py:395
  75.6 5.6 %collective-permute-start.7 = (bf16[64,5,4,128]{3,2,1,0:T(4,128)(2,1)S(1)}, bf16[64,5,4,128]{3,2,1,0:T(4,128)(2,1)S(1)}, u32[]{:S(2)}, u32[]{:S(2)}) collective-permute-start(bf16[64,5,4,128]{3,2,1,0:T(4,128)(2,1)S(1)} %all_to_all.10.mine_ref), channel_id=1, source_target_pairs={{0,2},{2,0},{1,3},{3,1},{4,6},{6,4},{5,7},{7,5},{8,10},{10,8},{9,1... | collective-permute-start | bytes 983048 | tf_op jit(solution)/shard_map/ppermute | solution.py:328

commit v4 on v3

--- a/solution.py
+++ b/solution.py
@@ -11,7 +11,7 @@
 F32 = jnp.float32
 BAND = ("xl", "z", "core")
 PEERS = ("tm", "xl", "z", "core")
-CHIPS = ("xl", "z", "tm")
+CHIPS = ("tm", "xl", "z")
 NT = (((1,), (1,)), ((), ()))
 
 
@@ -38,7 +38,7 @@
     ((384, 512), F32),
     ((2, 3, 6, 6, 16, 128), F32),
     ((6, 16, 128), F32),
-    ((1536, 128), F32),
+    ((1544, 128), F32),
     ((384, 512), BF),
     ((512, 384), F32),
     ((512, 512), BF),
@@ -169,7 +169,7 @@
 
     def relayout(i):
         cot_copy(i).wait()
-        cots[...] = cot[i].astype(F32).reshape(1536, 128)
+        cots[0:1536] = cot[i].astype(F32).reshape(1536, 128)
 
     def elements(h, pre):
         x = pre[:, h * 128 : h * 128 + 128]
@@ -305,12 +305,9 @@
     for i in range(3):
         mine = mine_ref[:, 2 + i].astype(F32)
         other = other_ref[:, 2 + i].astype(F32)
-        halves = (jnp.where(core == 0, mine, other), jnp.where(core == 0, other, mine))
-        for c in range(2):
-            for j in range(64):
-                top = c * 256 + (j & 15) * 16 + (j >> 4) * 4
-                if top < 432:
-                    wg_ref[top : top + 4, i * 128 : i * 128 + 128] = halves[c][j]
+        cols = slice(i * 128, i * 128 + 128)
+        wg_ref[0:256, cols] = jnp.where(core == 0, mine, other).reshape(256, 128)
+        wg_ref[256:432, cols] = jnp.where(core == 0, other, mine)[0:44].reshape(176, 128)
 
 
 def shifted(value, step):
@@ -400,7 +397,7 @@
         scratch=[pltpu.VMEM((128, 1024), BF), pltpu.VMEM((2, 4, 4, 16, 128), F32)],
         in_specs=[smem] + [vmem] * 7,
     )(core.reshape(1), grad, given, from_far, from_next, send, part, twin)
-    got = exchange(outgoing, ("tm", "xl", "z"))
+    got = exchange(outgoing, CHIPS)
     other = swapped(got)
     tokens, summed = call(
         take_body,

time: 83.5 us -> 83.5 us (level)
  no operation moved by 1% of the time
where the time goes in v4:
time: 83.5 us; the launch traced here: 83.1 us
  starting transfers between devices  33.5 us (40%)
  blocking collectives  19.5 us (23%)
  Pallas kernels  15.8 us (19%)
  waiting for transfers between devices  9.71 us (12%)
  local copies, waits for them, and re-layouts  3.57 us (4%)
    all_to_all x1, blocking collectives, exchange(): return lax.all_to_all(value, axes, split_axis=0, concat_axis=0, tiled=True)  19.5 us
    all_to_all x1, starting transfers between devices, exchange(): return lax.all_to_all(value, axes, split_axis=0, concat_axis=0, tiled=True)  12.5 us
    pallas_call x1, Pallas kernels, on_device(): call(main_body, tuple((jax.ShapeDtypeStruct(*out) for out in MAIN_OUTS)),...  9.7 us
    ppermute x2, starting transfers between devices, crossed(): return lax.ppermute(value, BAND, pairs + [(j, i) for i, j in pairs])  8.12 us
    ppermute x2, starting transfers between devices, shifted(): lax.ppermute(value, 'tm', [(i, i + step) for i in range(count) if 0 <= i...  5.33 us
    ppermute x3, starting transfers between devices, swapped(): return lax.ppermute(value, 'core', [(0, 1), (1, 0)])  5.04 us
    unnamed x7, local copies, waits for them, and re-layouts  3.53 us
    ppermute x2, waiting for transfers between devices, crossed(): return lax.ppermute(value, BAND, pairs + [(j, i) for i, j in pairs])  3.09 us
  transfers between devices with their start and end apart: 9, of which 5 were waited for; matrix products, arithmetic and copies ran while one was open for 0% of the time, Pallas kernels for 4%

profile of v4, /device:TPU:1, one launch (start us, length us, event | category | flops | bytes accessed | tf_op | source)
XLA Modules:
  0.0 83.1 jit_solution(325244536691284369)
XLA Ops:
  0.6 0.9 %copy.12 = bf16[2,16,4,4,128]{4,1,2,0,3:T(8,128)(2,1)S(1)} copy(bf16[2,16,4,4,128]{4,3,2,1,0:T(4,128)(2,1)} %param.5) | data formatting | bytes 262144 | tf_op args[0]
  1.6 4.0 %collective-permute-start = (bf16[4,2,2,16,128]{4,3,2,1,0:T(8,128)(2,1)S(1)}, bf16[4,2,2,16,128]{4,3,2,1,0:T(8,128)(2,1)S(1)}, u32[]{:S(2)}, u32[]{:S(2)}) collective-permute-start(bf16[4,2,2,16,128]{4,3,2,1,0:T(8,128)(2,1)S(1)} %slice.4), channel_id=1, source_target_pairs={{0,64},{64,128},{128,192},{1,65},{65,129},{129,193},{2,66},{66,130... | collective-permute-start | bytes 196616 | tf_op jit(solution)/shard_map/ppermute | solution.py:315
  5.6 0.0 copy-start
  5.7 1.0 %copy-done = bf16[384,432]{0,1:T(8,128)(2,1)S(1)} copy-done((bf16[384,432]{0,1:T(8,128)(2,1)S(1)}, bf16[384,432]{0,1:T(8,128)(2,1)}, u32[]{:S(2)}) %copy-start) | copy-done | bytes 331800
  6.6 0.0 copy-start.1
  6.6 0.7 copy-done.1
  7.3 1.3 %shard_map.68 = (bf16[384,512]{1,0:T(8,128)(2,1)S(1)}, bf16[432,384]{1,0:T(8,128)(2,1)S(1)}, s32[24]{0:T(128)S(1)}) custom-call(s32[1]{0:T(128)} %bitcast.2.me_ref, s32[2,16]{1,0:T(2,128)S(1)} %copy-done.1, bf16[432,384]{1,0:T(8,128)(2,1)S(1)} %bitcast.21), custom_call_target="tpu_custom_call" | custom-call | flops 1000000 | bytes 2000000 | tf_op jit(solution)/shard_map/pallas_call | solution.py:345
  8.6 0.0 collective-permute-done.prev
  8.7 4.4 %collective-permute-start.2 = (bf16[2,6,16,128]{3,2,1,0:T(8,128)(2,1)S(1)}, bf16[2,6,16,128]{3,2,1,0:T(8,128)(2,1)S(1)}, u32[]{:S(2)}, u32[]{:S(2)}) collective-permute-start(bf16[2,6,16,128]{3,2,1,0:T(8,128)(2,1)S(1)} %pad_maximum_fusion.1), channel_id=1, source_target_pairs={{2,4},{6,8},{10,12},{14,16},{18,20},{22,24},{26,28},{30,32},{34,36... | collective-permute-start | bytes 147464 | tf_op jit(solution)/shard_map/ppermute | solution.py:321
  13.1 0.1 collective-permute-start.1
  13.2 0.0 copy-start.2
  13.2 0.9 %copy-done.2 = s32[65536]{0:T(1024)S(1)} copy-done((s32[65536]{0:T(1024)S(1)}, s32[65536]{0:T(1024)}, u32[]{:S(2)}) %copy-start.2) | copy-done | bytes 262168
  14.2 1.6 %shard_map.69 = (s32[512,128]{1,0:T(8,128)S(1)}, s32[2,256,128]{2,1,0:T(8,128)S(1)}) custom-call(s32[1]{0:T(128)} %bitcast.2.me_ref, s32[512,128]{1,0:T(8,128)S(1)} %bitcast.22), custom_call_target="tpu_custom_call" | custom-call | flops 500000000 | bytes 2000000 | tf_op jit(solution)/shard_map/pallas_call | solution.py:362
  15.8 0.0 collective-permute-done.2.far
  15.8 0.0 collective-permute-done.1.near
  15.8 9.7 %shard_map.70 = (bf16[48,16,128]{2,1,0:T(8,128)(2,1)S(1)}, bf16[60,16,128]{2,1,0:T(8,128)(2,1)S(1)}, f32[2,4,4,16,128]{4,3,2,1,0:T(8,128)S(1)}, bf16[2,6,16,128]...) custom-call(s32[1]{0:T(128)} %bitcast.core_ref, s32[24]{0:T(128)S(1)} %get-tuple-element.19.mask_ref, ...), custom_call_target="tpu_custom_call" | custom-call | flops 4499999744 | bytes 5000000 | tf_op jit(solution)/shard_map/pallas_call | solution.py:371
  25.5 0.6 collective-permute-start.3
  26.1 1.1 %collective-permute-done.3.given_ref = bf16[60,16,128]{2,1,0:T(8,128)(2,1)S(1)} collective-permute-done((bf16[60,16,128]{2,1,0:T(8,128)(2,1)S(1)}, bf16[60,16,128]{2,1,0:T(8,128)(2,1)S(1)}, u32[]{:S(2)}, u32[]{:S(2)}) %collective-permute-start.3) | collective-permute-done | bytes 245792 | tf_op jit(solution)/shard_map/ppermute | solution.py:325
  27.2 0.8 shard_map.72
  28.0 12.5 %all-to-all-start = ((bf16[64,4,384]{2,1,0:T(4,128)(2,1)}), bf16[64,4,384]{2,1,0:T(4,128)(2,1)S(1)}, u32[]{:S(2)}, u32[]{:S(2)}) async-start(bf16[64,4,384]{2,1,0:T(4,128)(2,1)} %shard_map.72), calls=%async_computation | async-start | bytes 393216 | tf_op jit(solution)/shard_map/all_to_all | solution.py:329
  40.4 3.7 %collective-permute-start.4 = (bf16[2,6,16,128]{3,2,1,0:T(8,128)(2,1)S(1)}, bf16[2,6,16,128]{3,2,1,0:T(8,128)(2,1)S(1)}, u32[]{:S(2)}, u32[]{:S(2)}) collective-permute-start(bf16[2,6,16,128]{3,2,1,0:T(8,128)(2,1)S(1)} %get-tuple-element.27), channel_id=1, source_target_pairs={{2,4},{6,8},{10,12},{14,16},{18,20},{22,24},{26,28},{30,32},{34,36... | collective-permute-start | bytes 147464 | tf_op jit(solution)/shard_map/ppermute | solution.py:321
  44.2 3.1 %collective-permute-done.4.far_ref = bf16[2,6,16,128]{3,2,1,0:T(8,128)(2,1)S(1)} collective-permute-done((bf16[2,6,16,128]{3,2,1,0:T(8,128)(2,1)S(1)}, bf16[2,6,16,128]{3,2,1,0:T(8,128)(2,1)S(1)}, u32[]{:S(2)}, u32[]{:S(2)}) %collective-permute-start.4) | collective-permute-done | bytes 49184 | tf_op jit(solution)/shard_map/ppermute | solution.py:321
  47.3 1.3 %collective-permute-start.5 = (bf16[2,2,4,16,128]{4,3,2,1,0:T(8,128)(2,1)S(1)}, bf16[2,2,4,16,128]{4,3,2,1,0:T(8,128)(2,1)S(1)}, u32[]{:S(2)}, u32[]{:S(2)}) collective-permute-start(bf16[2,2,4,16,128]{4,3,2,1,0:T(8,128)(2,1)S(1)} %shard_map.71), channel_id=1, source_target_pairs={{64,0},{128,64},{192,128},{65,1},{129,65},{193,129},{66,2},{130,66... | collective-permute-start | bytes 196616 | tf_op jit(solution)/shard_map/ppermute | solution.py:315
  48.6 2.7 %all-to-all-done = bf16[64,4,384]{2,1,0:T(4,128)(2,1)S(1)} async-done(((bf16[64,4,384]{2,1,0:T(4,128)(2,1)}), bf16[64,4,384]{2,1,0:T(4,128)(2,1)S(1)}, u32[]{:S(2)}, u32[]{:S(2)}) %all-to-all-start) | async-done | bytes 196640 | tf_op jit(solution)/shard_map/all_to_all | solution.py:329
  51.3 0.1 convert_reduce_fusion.part_ref
  51.4 2.5 %collective-permute-start.6 = (f32[4,384]{1,0:T(4,128)S(1)}, f32[4,384]{1,0:T(4,128)S(1)}, u32[]{:S(2)}, u32[]{:S(2)}) collective-permute-start(f32[4,384]{1,0:T(4,128)S(1)} %convert_reduce_fusion.part_ref), channel_id=1, source_target_pairs={{0,1},{1,0},{2,3},{3,2},{4,5},{5,4},{6,7},{7,6},{8,9},{9,8},{10,11... | collective-permute-start | bytes 18440 | tf_op jit(solution)/shard_map/ppermute | solution.py:392
  53.9 0.0 collective-permute-done.5.next_ref
  53.9 1.5 %collective-permute-done.6.twin_ref = f32[4,384]{1,0:T(4,128)S(1)} collective-permute-done((f32[4,384]{1,0:T(4,128)S(1)}, f32[4,384]{1,0:T(4,128)S(1)}, u32[]{:S(2)}, u32[]{:S(2)}) %collective-permute-start.6) | collective-permute-done | bytes 6176 | tf_op jit(solution)/shard_map/ppermute | solution.py:392
  55.5 0.6 shard_map.73
  56.1 19.5 %all_to_all.10.mine_ref = bf16[64,5,4,128]{3,2,1,0:T(4,128)(2,1)S(1)} all-to-all(bf16[64,5,4,128]{3,2,1,0:T(4,128)(2,1)S(1)} %shard_map.73), channel_id=1, replica_groups=mesh['tm'=4,'xl'=2,'z'=8,'core'=2,'rep'=2] {'tm','xl','z'}, dimensions={0} | all-to-all | bytes 655360 | tf_op jit(solution)/shard_map/all_to_all | solution.py:329
  75.6 4.4 %collective-permute-start.7 = (bf16[64,5,4,128]{3,2,1,0:T(4,128)(2,1)S(1)}, bf16[64,5,4,128]{3,2,1,0:T(4,128)(2,1)S(1)}, u32[]{:S(2)}, u32[]{:S(2)}) collective-permute-start(bf16[64,5,4,128]{3,2,1,0:T(4,128)(2,1)S(1)} %all_to_all.10.mine_ref), channel_id=1, source_target_pairs={{0,2},{2,0},{1,3},{3,1},{4,6},{6,4},{5,7},{7,5},{8,10},{10,8},{9,1... | collective-permute-start | bytes 983048 | tf_op jit(solution)/shard_map/ppermute | solution.py:325
  80.0 1.3 %collective-permute-done.7.other_ref = bf16[64,5,4,128]{3,2,1,0:T(4,128)(2,1)S(1)} collective-permute-done((bf16[64,5,4,128]{3,2,1,0:T(4,128)(2,1)S(1)}, bf16[64,5,4,128]{3,2,1,0:T(4,128)(2,1)S(1)}, u32[]{:S(2)}, u32[]{:S(2)}) %collective-permute-start.7) | collective-permute-done | bytes 327712 | tf_op jit(solution)/shard_map/ppermute | solution.py:325
  81.2 1.9 %shard_map.74 = (bf16[2,256,128]{2,1,0:T(8,128)(2,1)}, f32[432,384]{1,0:T(8,128)}) custom-call(s32[1]{0:T(128)} %bitcast.core_ref, bf16[64,5,4,128]{3,2,1,0:T(4,128)(2,1)S(1)} %all_to_all.10.mine_ref, bf16[64,5,4,128]{3,2,1,0:T(4,128)(2,1)S(1)} %collective-permute-done.7.other_ref, s32[2,256,128]{2,1,0:T(8,128)S(1)} %get-tuple-element.31.take_ref), custom_call_target="tpu_custom_call" | custom-call | flops 200000000 | bytes 1000000 | tf_op jit(solution)/shard_map/pallas_call | solution.py:402
  (6 shorter events, 0.1 us)
Async XLA Ops:
  1.6 7.1 %collective-permute-start = (bf16[4,2,2,16,128]{4,3,2,1,0:T(8,128)(2,1)S(1)}, bf16[4,2,2,16,128]{4,3,2,1,0:T(8,128)(2,1)S(1)}, u32[]{:S(2)}, u32[]{:S(2)}) collective-permute-start(bf16[4,2,2,16,128]{4,3,2,1,0:T(8,128)(2,1)S(1)} %slice.4), channel_id=1, source_target_pairs={{0,64},{64,128},{128,192},{1,65},{65,129},{129,193},{2,66},{66,130... | collective-permute-start | bytes 196616 | tf_op jit(solution)/shard_map/ppermute | solution.py:315
  5.6 1.0 %copy-start = (bf16[384,432]{0,1:T(8,128)(2,1)S(1)}, bf16[384,432]{0,1:T(8,128)(2,1)}, u32[]{:S(2)}) copy-start(bf16[384,432]{0,1:T(8,128)(2,1)} %param.6) | copy-start | bytes 995332
  6.6 0.7 copy-start.1
  8.7 7.1 %collective-permute-start.2 = (bf16[2,6,16,128]{3,2,1,0:T(8,128)(2,1)S(1)}, bf16[2,6,16,128]{3,2,1,0:T(8,128)(2,1)S(1)}, u32[]{:S(2)}, u32[]{:S(2)}) collective-permute-start(bf16[2,6,16,128]{3,2,1,0:T(8,128)(2,1)S(1)} %pad_maximum_fusion.1), channel_id=1, source_target_pairs={{2,4},{6,8},{10,12},{14,16},{18,20},{22,24},{26,28},{30,32},{34,36... | collective-permute-start | bytes 147464 | tf_op jit(solution)/shard_map/ppermute | solution.py:321
  13.1 2.7 %collective-permute-start.1 = (bf16[2,6,16,128]{3,2,1,0:T(8,128)(2,1)S(1)}, bf16[2,6,16,128]{3,2,1,0:T(8,128)(2,1)S(1)}, u32[]{:S(2)}, u32[]{:S(2)}) collective-permute-start(bf16[2,6,16,128]{3,2,1,0:T(8,128)(2,1)S(1)} %pad_maximum_fusion), channel_id=1, source_target_pairs={{0,2},{2,0},{1,3},{3,1},{4,6},{6,4},{5,7},{7,5},{8,10},{10,8},{9,1... | collective-permute-start | bytes 147464 | tf_op jit(solution)/shard_map/ppermute | solution.py:325
  13.2 1.0 %copy-start.2 = (s32[65536]{0:T(1024)S(1)}, s32[65536]{0:T(1024)}, u32[]{:S(2)}) copy-start(s32[65536]{0:T(1024)} %param.9) | copy-start | bytes 786436
  25.5 1.7 %collective-permute-start.3 = (bf16[60,16,128]{2,1,0:T(8,128)(2,1)S(1)}, bf16[60,16,128]{2,1,0:T(8,128)(2,1)S(1)}, u32[]{:S(2)}, u32[]{:S(2)}) collective-permute-start(bf16[60,16,128]{2,1,0:T(8,128)(2,1)S(1)} %get-tuple-element.26), channel_id=1, source_target_pairs={{0,2},{2,0},{1,3},{3,1},{4,6},{6,4},{5,7},{7,5},{8,10},{10,8},{9,1... | collective-permute-start | bytes 737288 | tf_op jit(solution)/shard_map/ppermute | solution.py:325
  28.0 23.3 %all-to-all-start = ((bf16[64,4,384]{2,1,0:T(4,128)(2,1)}), bf16[64,4,384]{2,1,0:T(4,128)(2,1)S(1)}, u32[]{:S(2)}, u32[]{:S(2)}) async-start(bf16[64,4,384]{2,1,0:T(4,128)(2,1)} %shard_map.72), calls=%async_computation | async-start | bytes 393216 | tf_op jit(solution)/shard_map/all_to_all | solution.py:329
  40.4 6.8 %collective-permute-start.4 = (bf16[2,6,16,128]{3,2,1,0:T(8,128)(2,1)S(1)}, bf16[2,6,16,128]{3,2,1,0:T(8,128)(2,1)S(1)}, u32[]{:S(2)}, u32[]{:S(2)}) collective-permute-start(bf16[2,6,16,128]{3,2,1,0:T(8,128)(2,1)S(1)} %get-tuple-element.27), channel_id=1, source_target_pairs={{2,4},{6,8},{10,12},{14,16},{18,20},{22,24},{26,28},{30,32},{34,36... | collective-permute-start | bytes 147464 | tf_op jit(solution)/shard_map/ppermute | solution.py:321
  47.3 6.7 %collective-permute-start.5 = (bf16[2,2,4,16,128]{4,3,2,1,0:T(8,128)(2,1)S(1)}, bf16[2,2,4,16,128]{4,3,2,1,0:T(8,128)(2,1)S(1)}, u32[]{:S(2)}, u32[]{:S(2)}) collective-permute-start(bf16[2,2,4,16,128]{4,3,2,1,0:T(8,128)(2,1)S(1)} %shard_map.71), channel_id=1, source_target_pairs={{64,0},{128,64},{192,128},{65,1},{129,65},{193,129},{66,2},{130,66... | collective-permute-start | bytes 196616 | tf_op jit(solution)/shard_map/ppermute | solution.py:315
  51.4 4.1 %collective-permute-start.6 = (f32[4,384]{1,0:T(4,128)S(1)}, f32[4,384]{1,0:T(4,128)S(1)}, u32[]{:S(2)}, u32[]{:S(2)}) collective-permute-start(f32[4,384]{1,0:T(4,128)S(1)} %convert_reduce_fusion.part_ref), channel_id=1, source_target_pairs={{0,1},{1,0},{2,3},{3,2},{4,5},{5,4},{6,7},{7,6},{8,9},{9,8},{10,11... | collective-permute-start | bytes 18440 | tf_op jit(solution)/shard_map/ppermute | solution.py:392
  75.6 5.6 %collective-permute-start.7 = (bf16[64,5,4,128]{3,2,1,0:T(4,128)(2,1)S(1)}, bf16[64,5,4,128]{3,2,1,0:T(4,128)(2,1)S(1)}, u32[]{:S(2)}, u32[]{:S(2)}) collective-permute-start(bf16[64,5,4,128]{3,2,1,0:T(4,128)(2,1)S(1)} %all_to_all.10.mine_ref), channel_id=1, source_target_pairs={{0,2},{2,0},{1,3},{3,1},{4,6},{6,4},{5,7},{7,5},{8,10},{10,8},{9,1... | collective-permute-start | bytes 983048 | tf_op jit(solution)/shard_map/ppermute | solution.py:325

commit v5 on v4

--- a/solution.py
+++ b/solution.py
@@ -283,25 +283,36 @@
         out_ref[:, 2 + i] = jnp.broadcast_to(piece[None], (64, 4, 128))
 
 
-def take_body(core_ref, mine_ref, other_ref, take_ref, out_ref, wg_ref):
-    core = core_ref[0]
-    got = jnp.concatenate([ref[:, core].astype(F32).reshape(256, 128) for ref in (mine_ref, other_ref)]).astype(BF)
+def taken(core, rows_ref, take_ref, first):
+    got = rows_ref[:, core].astype(F32).reshape(256, 128).astype(BF)
     src = lax.broadcasted_iota(jnp.int32, (128, 128), 0)
     dst = lax.broadcasted_iota(jnp.int32, (128, 128), 1)
     lane = lax.broadcasted_iota(jnp.int32, (256, 128), 1)
     want = ((dst & 1) << 6) + (((dst >> 1) & 1) << 4) + ((dst >> 2) & 15)
     takes = []
     for e in range(2):
-        row = take_ref[e]
-        takes.append(jnp.concatenate([ones_where(row == lane + i * 128) for i in range(4)], axis=1))
+        row = take_ref[e] - first
+        takes.append(jnp.concatenate([ones_where(row == lane + i * 128) for i in range(2)], axis=1))
+    result = []
     for b in range(2):
         total = None
         for e in range(2):
             place = ones_where((src == want + b * 32) & ((dst >> 6) == e))
-            moved = matmul(got, place).astype(BF)
-            term = matmul(takes[e], moved)
+            term = matmul(takes[e], matmul(got, place).astype(BF))
             total = term if total is None else total + term
-        out_ref[b] = total.astype(BF)
+        result.append(total)
+    return result
+
+
+def own_body(core_ref, mine_ref, take_ref, part_ref):
+    for b, x in enumerate(taken(core_ref[0], mine_ref, take_ref, 0)):
+        part_ref[b] = x.astype(BF)
+
+
+def take_body(core_ref, mine_ref, other_ref, take_ref, part_ref, out_ref, wg_ref):
+    core = core_ref[0]
+    for b, x in enumerate(taken(core, other_ref, take_ref, 256)):
+        out_ref[b] = (part_ref[b].astype(F32) + x).astype(BF)
     for i in range(3):
         mine = mine_ref[:, 2 + i].astype(F32)
         other = other_ref[:, 2 + i].astype(F32)
@@ -399,12 +410,18 @@
     )(core.reshape(1), grad, given, from_far, from_next, send, part, twin)
     got = exchange(outgoing, CHIPS)
     other = swapped(got)
+    part = call(
+        own_body,
+        jax.ShapeDtypeStruct((2, 256, 128), BF),
+        (100e6, 1e6),
+        in_specs=[smem] + [vmem] * 2,
+    )(core.reshape(1), got, take)
     tokens, summed = call(
         take_body,
         (jax.ShapeDtypeStruct((2, 256, 128), BF), jax.ShapeDtypeStruct((432, 384), F32)),
         (200e6, 1e6),
-        in_specs=[smem] + [vmem] * 3,
-    )(core.reshape(1), got, other, take)
+        in_specs=[smem] + [vmem] * 4,
+    )(core.reshape(1), got, other, take, part)
     return tokens, summed.T
 
 

time: 83.5 us -> 83.3 us (level)
  no operation moved by 1% of the time
where the time goes in v5:
time: 83.3 us; the launch traced here: 82.9 us
  starting transfers between devices  33.5 us (40%)
  blocking collectives  19.5 us (23%)
  Pallas kernels  16.3 us (20%)
  waiting for transfers between devices  9.08 us (11%)
  local copies, waits for them, and re-layouts  3.57 us (4%)
    all_to_all x1, blocking collectives, exchange(): return lax.all_to_all(value, axes, split_axis=0, concat_axis=0, tiled=True)  19.5 us
    all_to_all x1, starting transfers between devices, exchange(): return lax.all_to_all(value, axes, split_axis=0, concat_axis=0, tiled=True)  12.5 us
    pallas_call x1, Pallas kernels, on_device(): call(main_body, tuple((jax.ShapeDtypeStruct(*out) for out in MAIN_OUTS)),...  9.7 us
    ppermute x2, starting transfers between devices, crossed(): return lax.ppermute(value, BAND, pairs + [(j, i) for i, j in pairs])  8.12 us
    ppermute x2, starting transfers between devices, shifted(): lax.ppermute(value, 'tm', [(i, i + step) for i in range(count) if 0 <= i...  5.33 us
    ppermute x3, starting transfers between devices, swapped(): return lax.ppermute(value, 'core', [(0, 1), (1, 0)])  5.04 us
    unnamed x7, local copies, waits for them, and re-layouts  3.53 us
    ppermute x2, waiting for transfers between devices, crossed(): return lax.ppermute(value, BAND, pairs + [(j, i) for i, j in pairs])  3.09 us
  transfers between devices with their start and end apart: 9, of which 5 were waited for; matrix products, arithmetic and copies ran while one was open for 0% of the time, Pallas kernels for 4%

profile of v5, /device:TPU:1, one launch (start us, length us, event | category | flops | bytes accessed | tf_op | source)
XLA Modules:
  0.0 82.9 jit_solution(2675987415593526128)
XLA Ops:
  0.6 0.9 %copy.12 = bf16[2,16,4,4,128]{4,1,2,0,3:T(8,128)(2,1)S(1)} copy(bf16[2,16,4,4,128]{4,3,2,1,0:T(4,128)(2,1)} %param.5) | data formatting | bytes 262144 | tf_op args[0]
  1.6 4.0 %collective-permute-start = (bf16[4,2,2,16,128]{4,3,2,1,0:T(8,128)(2,1)S(1)}, bf16[4,2,2,16,128]{4,3,2,1,0:T(8,128)(2,1)S(1)}, u32[]{:S(2)}, u32[]{:S(2)}) collective-permute-start(bf16[4,2,2,16,128]{4,3,2,1,0:T(8,128)(2,1)S(1)} %slice.4), channel_id=1, source_target_pairs={{0,64},{64,128},{128,192},{1,65},{65,129},{129,193},{2,66},{66,130... | collective-permute-start | bytes 196616 | tf_op jit(solution)/shard_map/ppermute | solution.py:326
  5.6 0.0 copy-start
  5.7 1.0 %copy-done = bf16[384,432]{0,1:T(8,128)(2,1)S(1)} copy-done((bf16[384,432]{0,1:T(8,128)(2,1)S(1)}, bf16[384,432]{0,1:T(8,128)(2,1)}, u32[]{:S(2)}) %copy-start) | copy-done | bytes 331800
  6.6 0.0 copy-start.1
  6.6 0.7 copy-done.1
  7.3 1.3 %shard_map.68 = (bf16[384,512]{1,0:T(8,128)(2,1)S(1)}, bf16[432,384]{1,0:T(8,128)(2,1)S(1)}, s32[24]{0:T(128)S(1)}) custom-call(s32[1]{0:T(128)} %bitcast.2.me_ref, s32[2,16]{1,0:T(2,128)S(1)} %copy-done.1, bf16[432,384]{1,0:T(8,128)(2,1)S(1)} %bitcast.21), custom_call_target="tpu_custom_call" | custom-call | flops 1000000 | bytes 2000000 | tf_op jit(solution)/shard_map/pallas_call | solution.py:356
  8.6 0.0 collective-permute-done.prev
  8.7 4.4 %collective-permute-start.2 = (bf16[2,6,16,128]{3,2,1,0:T(8,128)(2,1)S(1)}, bf16[2,6,16,128]{3,2,1,0:T(8,128)(2,1)S(1)}, u32[]{:S(2)}, u32[]{:S(2)}) collective-permute-start(bf16[2,6,16,128]{3,2,1,0:T(8,128)(2,1)S(1)} %pad_maximum_fusion.1), channel_id=1, source_target_pairs={{2,4},{6,8},{10,12},{14,16},{18,20},{22,24},{26,28},{30,32},{34,36... | collective-permute-start | bytes 147464 | tf_op jit(solution)/shard_map/ppermute | solution.py:332
  13.1 0.1 collective-permute-start.1
  13.2 0.0 copy-start.2
  13.2 0.9 %copy-done.2 = s32[65536]{0:T(1024)S(1)} copy-done((s32[65536]{0:T(1024)S(1)}, s32[65536]{0:T(1024)}, u32[]{:S(2)}) %copy-start.2) | copy-done | bytes 262168
  14.2 1.6 %shard_map.69 = (s32[512,128]{1,0:T(8,128)S(1)}, s32[2,256,128]{2,1,0:T(8,128)S(1)}) custom-call(s32[1]{0:T(128)} %bitcast.2.me_ref, s32[512,128]{1,0:T(8,128)S(1)} %bitcast.22), custom_call_target="tpu_custom_call" | custom-call | flops 500000000 | bytes 2000000 | tf_op jit(solution)/shard_map/pallas_call | solution.py:373
  15.8 0.0 collective-permute-done.2.far
  15.8 0.0 collective-permute-done.1.near
  15.8 9.7 %shard_map.70 = (bf16[48,16,128]{2,1,0:T(8,128)(2,1)S(1)}, bf16[60,16,128]{2,1,0:T(8,128)(2,1)S(1)}, f32[2,4,4,16,128]{4,3,2,1,0:T(8,128)S(1)}, bf16[2,6,16,128]...) custom-call(s32[1]{0:T(128)} %bitcast.core_ref, s32[24]{0:T(128)S(1)} %get-tuple-element.19.mask_ref, ...), custom_call_target="tpu_custom_call" | custom-call | flops 4499999744 | bytes 5000000 | tf_op jit(solution)/shard_map/pallas_call | solution.py:382
  25.5 0.6 collective-permute-start.3
  26.1 1.1 %collective-permute-done.3.given_ref = bf16[60,16,128]{2,1,0:T(8,128)(2,1)S(1)} collective-permute-done((bf16[60,16,128]{2,1,0:T(8,128)(2,1)S(1)}, bf16[60,16,128]{2,1,0:T(8,128)(2,1)S(1)}, u32[]{:S(2)}, u32[]{:S(2)}) %collective-permute-start.3) | collective-permute-done | bytes 245792 | tf_op jit(solution)/shard_map/ppermute | solution.py:336
  27.2 0.8 shard_map.72
  28.0 12.5 %all-to-all-start = ((bf16[64,4,384]{2,1,0:T(4,128)(2,1)}), bf16[64,4,384]{2,1,0:T(4,128)(2,1)S(1)}, u32[]{:S(2)}, u32[]{:S(2)}) async-start(bf16[64,4,384]{2,1,0:T(4,128)(2,1)} %shard_map.72), calls=%async_computation | async-start | bytes 393216 | tf_op jit(solution)/shard_map/all_to_all | solution.py:340
  40.4 3.7 %collective-permute-start.4 = (bf16[2,6,16,128]{3,2,1,0:T(8,128)(2,1)S(1)}, bf16[2,6,16,128]{3,2,1,0:T(8,128)(2,1)S(1)}, u32[]{:S(2)}, u32[]{:S(2)}) collective-permute-start(bf16[2,6,16,128]{3,2,1,0:T(8,128)(2,1)S(1)} %get-tuple-element.27), channel_id=1, source_target_pairs={{2,4},{6,8},{10,12},{14,16},{18,20},{22,24},{26,28},{30,32},{34,36... | collective-permute-start | bytes 147464 | tf_op jit(solution)/shard_map/ppermute | solution.py:332
  44.2 3.1 %collective-permute-done.4.far_ref = bf16[2,6,16,128]{3,2,1,0:T(8,128)(2,1)S(1)} collective-permute-done((bf16[2,6,16,128]{3,2,1,0:T(8,128)(2,1)S(1)}, bf16[2,6,16,128]{3,2,1,0:T(8,128)(2,1)S(1)}, u32[]{:S(2)}, u32[]{:S(2)}) %collective-permute-start.4) | collective-permute-done | bytes 49184 | tf_op jit(solution)/shard_map/ppermute | solution.py:332
  47.3 1.3 %collective-permute-start.5 = (bf16[2,2,4,16,128]{4,3,2,1,0:T(8,128)(2,1)S(1)}, bf16[2,2,4,16,128]{4,3,2,1,0:T(8,128)(2,1)S(1)}, u32[]{:S(2)}, u32[]{:S(2)}) collective-permute-start(bf16[2,2,4,16,128]{4,3,2,1,0:T(8,128)(2,1)S(1)} %shard_map.71), channel_id=1, source_target_pairs={{64,0},{128,64},{192,128},{65,1},{129,65},{193,129},{66,2},{130,66... | collective-permute-start | bytes 196616 | tf_op jit(solution)/shard_map/ppermute | solution.py:326
  48.6 2.7 %all-to-all-done = bf16[64,4,384]{2,1,0:T(4,128)(2,1)S(1)} async-done(((bf16[64,4,384]{2,1,0:T(4,128)(2,1)}), bf16[64,4,384]{2,1,0:T(4,128)(2,1)S(1)}, u32[]{:S(2)}, u32[]{:S(2)}) %all-to-all-start) | async-done | bytes 196640 | tf_op jit(solution)/shard_map/all_to_all | solution.py:340
  51.3 0.1 convert_reduce_fusion.part_ref
  51.4 2.5 %collective-permute-start.6 = (f32[4,384]{1,0:T(4,128)S(1)}, f32[4,384]{1,0:T(4,128)S(1)}, u32[]{:S(2)}, u32[]{:S(2)}) collective-permute-start(f32[4,384]{1,0:T(4,128)S(1)} %convert_reduce_fusion.part_ref), channel_id=1, source_target_pairs={{0,1},{1,0},{2,3},{3,2},{4,5},{5,4},{6,7},{7,6},{8,9},{9,8},{10,11... | collective-permute-start | bytes 18440 | tf_op jit(solution)/shard_map/ppermute | solution.py:403
  53.9 0.0 collective-permute-done.5.next_ref
  53.9 1.5 %collective-permute-done.6.twin_ref = f32[4,384]{1,0:T(4,128)S(1)} collective-permute-done((f32[4,384]{1,0:T(4,128)S(1)}, f32[4,384]{1,0:T(4,128)S(1)}, u32[]{:S(2)}, u32[]{:S(2)}) %collective-permute-start.6) | collective-permute-done | bytes 6176 | tf_op jit(solution)/shard_map/ppermute | solution.py:403
  55.5 0.6 shard_map.73
  56.1 19.5 %all_to_all.10.mine_ref = bf16[64,5,4,128]{3,2,1,0:T(4,128)(2,1)S(1)} all-to-all(bf16[64,5,4,128]{3,2,1,0:T(4,128)(2,1)S(1)} %shard_map.73), channel_id=1, replica_groups=mesh['tm'=4,'xl'=2,'z'=8,'core'=2,'rep'=2] {'tm','xl','z'}, dimensions={0} | all-to-all | bytes 655360 | tf_op jit(solution)/shard_map/all_to_all | solution.py:340
  75.6 4.4 %collective-permute-start.7 = (bf16[64,5,4,128]{3,2,1,0:T(4,128)(2,1)S(1)}, bf16[64,5,4,128]{3,2,1,0:T(4,128)(2,1)S(1)}, u32[]{:S(2)}, u32[]{:S(2)}) collective-permute-start(bf16[64,5,4,128]{3,2,1,0:T(4,128)(2,1)S(1)} %all_to_all.10.mine_ref), channel_id=1, source_target_pairs={{0,2},{2,0},{1,3},{3,1},{4,6},{6,4},{5,7},{7,5},{8,10},{10,8},{9,1... | collective-permute-start | bytes 983048 | tf_op jit(solution)/shard_map/ppermute | solution.py:336
  80.0 0.6 shard_map.74.part_ref
  80.6 0.6 collective-permute-done.7.other_ref
  81.2 1.7 %shard_map.75 = (bf16[2,256,128]{2,1,0:T(8,128)(2,1)}, f32[432,384]{1,0:T(8,128)}) custom-call(s32[1]{0:T(128)} %bitcast.core_ref, bf16[64,5,4,128]{3,2,1,0:T(4,128)(2,1)S(1)} %all_to_all.10.mine_ref, bf16[64,5,4,128]{3,2,1,0:T(4,128)(2,1)S(1)} %collective-permute-done.7.other_ref, s32[2,256,128]{2,1,0:T(8,128)S(1)} %get-tuple-element.31.take_ref, ...), custom_call_target="tpu_custom_call" | custom-call | flops 200000000 | bytes 1000000 | tf_op jit(solution)/shard_map/pallas_call | solution.py:419
  (6 shorter events, 0.1 us)
Async XLA Ops:
  1.6 7.1 %collective-permute-start = (bf16[4,2,2,16,128]{4,3,2,1,0:T(8,128)(2,1)S(1)}, bf16[4,2,2,16,128]{4,3,2,1,0:T(8,128)(2,1)S(1)}, u32[]{:S(2)}, u32[]{:S(2)}) collective-permute-start(bf16[4,2,2,16,128]{4,3,2,1,0:T(8,128)(2,1)S(1)} %slice.4), channel_id=1, source_target_pairs={{0,64},{64,128},{128,192},{1,65},{65,129},{129,193},{2,66},{66,130... | collective-permute-start | bytes 196616 | tf_op jit(solution)/shard_map/ppermute | solution.py:326
  5.6 1.0 %copy-start = (bf16[384,432]{0,1:T(8,128)(2,1)S(1)}, bf16[384,432]{0,1:T(8,128)(2,1)}, u32[]{:S(2)}) copy-start(bf16[384,432]{0,1:T(8,128)(2,1)} %param.6) | copy-start | bytes 995332
  6.6 0.7 copy-start.1
  8.7 7.1 %collective-permute-start.2 = (bf16[2,6,16,128]{3,2,1,0:T(8,128)(2,1)S(1)}, bf16[2,6,16,128]{3,2,1,0:T(8,128)(2,1)S(1)}, u32[]{:S(2)}, u32[]{:S(2)}) collective-permute-start(bf16[2,6,16,128]{3,2,1,0:T(8,128)(2,1)S(1)} %pad_maximum_fusion.1), channel_id=1, source_target_pairs={{2,4},{6,8},{10,12},{14,16},{18,20},{22,24},{26,28},{30,32},{34,36... | collective-permute-start | bytes 147464 | tf_op jit(solution)/shard_map/ppermute | solution.py:332
  13.1 2.7 %collective-permute-start.1 = (bf16[2,6,16,128]{3,2,1,0:T(8,128)(2,1)S(1)}, bf16[2,6,16,128]{3,2,1,0:T(8,128)(2,1)S(1)}, u32[]{:S(2)}, u32[]{:S(2)}) collective-permute-start(bf16[2,6,16,128]{3,2,1,0:T(8,128)(2,1)S(1)} %pad_maximum_fusion), channel_id=1, source_target_pairs={{0,2},{2,0},{1,3},{3,1},{4,6},{6,4},{5,7},{7,5},{8,10},{10,8},{9,1... | collective-permute-start | bytes 147464 | tf_op jit(solution)/shard_map/ppermute | solution.py:336
  13.2 1.0 %copy-start.2 = (s32[65536]{0:T(1024)S(1)}, s32[65536]{0:T(1024)}, u32[]{:S(2)}) copy-start(s32[65536]{0:T(1024)} %param.9) | copy-start | bytes 786436
  25.5 1.7 %collective-permute-start.3 = (bf16[60,16,128]{2,1,0:T(8,128)(2,1)S(1)}, bf16[60,16,128]{2,1,0:T(8,128)(2,1)S(1)}, u32[]{:S(2)}, u32[]{:S(2)}) collective-permute-start(bf16[60,16,128]{2,1,0:T(8,128)(2,1)S(1)} %get-tuple-element.26), channel_id=1, source_target_pairs={{0,2},{2,0},{1,3},{3,1},{4,6},{6,4},{5,7},{7,5},{8,10},{10,8},{9,1... | collective-permute-start | bytes 737288 | tf_op jit(solution)/shard_map/ppermute | solution.py:336
  28.0 23.3 %all-to-all-start = ((bf16[64,4,384]{2,1,0:T(4,128)(2,1)}), bf16[64,4,384]{2,1,0:T(4,128)(2,1)S(1)}, u32[]{:S(2)}, u32[]{:S(2)}) async-start(bf16[64,4,384]{2,1,0:T(4,128)(2,1)} %shard_map.72), calls=%async_computation | async-start | bytes 393216 | tf_op jit(solution)/shard_map/all_to_all | solution.py:340
  40.4 6.8 %collective-permute-start.4 = (bf16[2,6,16,128]{3,2,1,0:T(8,128)(2,1)S(1)}, bf16[2,6,16,128]{3,2,1,0:T(8,128)(2,1)S(1)}, u32[]{:S(2)}, u32[]{:S(2)}) collective-permute-start(bf16[2,6,16,128]{3,2,1,0:T(8,128)(2,1)S(1)} %get-tuple-element.27), channel_id=1, source_target_pairs={{2,4},{6,8},{10,12},{14,16},{18,20},{22,24},{26,28},{30,32},{34,36... | collective-permute-start | bytes 147464 | tf_op jit(solution)/shard_map/ppermute | solution.py:332
  47.3 6.7 %collective-permute-start.5 = (bf16[2,2,4,16,128]{4,3,2,1,0:T(8,128)(2,1)S(1)}, bf16[2,2,4,16,128]{4,3,2,1,0:T(8,128)(2,1)S(1)}, u32[]{:S(2)}, u32[]{:S(2)}) collective-permute-start(bf16[2,2,4,16,128]{4,3,2,1,0:T(8,128)(2,1)S(1)} %shard_map.71), channel_id=1, source_target_pairs={{64,0},{128,64},{192,128},{65,1},{129,65},{193,129},{66,2},{130,66... | collective-permute-start | bytes 196616 | tf_op jit(solution)/shard_map/ppermute | solution.py:326
  51.4 4.1 %collective-permute-start.6 = (f32[4,384]{1,0:T(4,128)S(1)}, f32[4,384]{1,0:T(4,128)S(1)}, u32[]{:S(2)}, u32[]{:S(2)}) collective-permute-start(f32[4,384]{1,0:T(4,128)S(1)} %convert_reduce_fusion.part_ref), channel_id=1, source_target_pairs={{0,1},{1,0},{2,3},{3,2},{4,5},{5,4},{6,7},{7,6},{8,9},{9,8},{10,11... | collective-permute-start | bytes 18440 | tf_op jit(solution)/shard_map/ppermute | solution.py:403
  75.6 5.6 %collective-permute-start.7 = (bf16[64,5,4,128]{3,2,1,0:T(4,128)(2,1)S(1)}, bf16[64,5,4,128]{3,2,1,0:T(4,128)(2,1)S(1)}, u32[]{:S(2)}, u32[]{:S(2)}) collective-permute-start(bf16[64,5,4,128]{3,2,1,0:T(4,128)(2,1)S(1)} %all_to_all.10.mine_ref), channel_id=1, source_target_pairs={{0,2},{2,0},{1,3},{3,1},{4,6},{6,4},{5,7},{7,5},{8,10},{10,8},{9,1... | collective-permute-start | bytes 983048 | tf_op jit(solution)/shard_map/ppermute | solution.py:336
